TPU v7x, 256 devices: a whole 4x4x8 slice. The times are simulated.
256 devices in a mesh: row: 8 (over z), col: 32 (over y, x, core).
Axes of the slice: x: 4, y: 4, z: 8, core: 2. Of those that a mesh axis runs over, the one named last changes fastest.
Arguments:
- tokens: bfloat16 [1536, 4096], P('row', 'col'), may hold values from -6 to 6
- w_in: bfloat16 [4096, 12288], P('row', 'col'), may hold values from -0.09375 to 0.09375
- bias_in: float32 [12288], P('col'), may hold values from -3 to 3
- w_out: bfloat16 [12288, 4096], P('row', 'col'), may hold values from -0.0546875 to 0.0546875
- grad_out: bfloat16 [1536, 4096], P('row', 'col'), may hold values from -1.5 to 1.5
Outputs:
- block_out: bfloat16 [1536, 4096], P('row', 'col')
- grad_tokens: bfloat16 [1536, 4096], P('row', 'col')
- grad_w_in: float32 [4096, 12288], P('row', 'col')
- grad_bias: float32 [12288], P('col')
- grad_w_out: float32 [12288, 4096], P('row', 'col')
All inputs are finite; a program needn't handle non-finite values.
Results may differ from a plain program's by a relative error of at most 0.029.
Values may be sent and summed in bfloat16 or wider, within the bound.
A program may use at most 64 MiB of HBM per device.

v0:
```python
import jax
import jax.numpy as jnp
from jax import lax
from jax.sharding import PartitionSpec as P


def gelu_grad(preact, upstream):
    return jax.vjp(jax.nn.gelu, preact)[1](upstream)[0]


def contract_rows(left, right):
    return lax.dot_general(
        left, right, (((0,), (0,)), ((), ())), preferred_element_type=jnp.float32
    )


def contract_cols(left, right):
    return lax.dot_general(
        left, right, (((1,), (1,)), ((), ())), preferred_element_type=jnp.float32
    )


def per_device(tokens, w_in, bias_in, w_out, grad_out):
    all_features = lax.all_gather(tokens, "col", axis=1, tiled=True)
    in_columns = lax.all_gather(w_in, "row", axis=0, tiled=True)
    preact = jnp.dot(all_features, in_columns, preferred_element_type=jnp.float32) + bias_in
    hidden = jax.nn.gelu(preact).astype(jnp.bfloat16)
    all_hidden = lax.all_gather(hidden, "col", axis=1, tiled=True)
    out_columns = lax.all_gather(w_out, "row", axis=0, tiled=True)
    block_out = jnp.dot(all_hidden, out_columns, preferred_element_type=jnp.float32).astype(
        jnp.bfloat16
    )
    window = out_columns
    hidden_sums = lax.psum_scatter(
        contract_cols(window, grad_out).astype(jnp.bfloat16), "col", scatter_dimension=0, tiled=True
    ).astype(jnp.float32)
    grad_pre = gelu_grad(preact, hidden_sums.T).astype(jnp.bfloat16)
    window = in_columns
    input_sums = lax.psum_scatter(
        contract_cols(window, grad_pre).astype(jnp.bfloat16), "col", scatter_dimension=0, tiled=True
    ).astype(jnp.float32)
    grad_tokens = input_sums.T.astype(jnp.bfloat16)
    grad_bias = lax.psum(jnp.sum(grad_pre, axis=0, dtype=jnp.float32), "row")
    window = all_features
    grad_w_in = lax.psum_scatter(
        contract_rows(window, grad_pre).astype(jnp.bfloat16), "row", scatter_dimension=0, tiled=True
    ).astype(jnp.float32)
    window = all_hidden
    grad_w_out = lax.psum_scatter(
        contract_rows(window, grad_out).astype(jnp.bfloat16), "row", scatter_dimension=0, tiled=True
    ).astype(jnp.float32)
    return (block_out, grad_tokens, grad_w_in, grad_bias, grad_w_out)


def solution(mesh):
    return jax.shard_map(
        per_device,
        mesh=mesh,
        in_specs=(P("row", "col"), P("row", "col"), P("col"), P("row", "col"), P("row", "col")),
        out_specs=(P("row", "col"), P("row", "col"), P("row", "col"), P("col"), P("row", "col")),
        check_vma=False,
    )
```

profile of v0, /device:TPU:96, one launch (start us, length us, event | category | flops | bytes accessed | tf_op | source)
XLA Modules:
  0.0 515.0 jit_solution(3191797090625105020)
XLA Ops:
  7.2 0.0 copy-start
  7.2 0.0 all-gather.11.cloned.1.call-start
  7.2 0.7 all-gather.11.cloned.1.call-update
  7.9 0.0 reduce-scatter.13.cloned.1.call-start
  8.0 48.2 %all-gather.11.cloned.1.call-done = bf16[12288,128]{1,0:T(8,128)(2,1)} async-done(((bf16[1536,128]{1,0:T(8,128)(2,1)}), bf16[12288,128]{1,0:T(8,128)(2,1)}) %all-gather.11.cloned.1.call-update) | async-done | bytes 3145744 | tf_op jit(solution)/shard_map/all_gather | solution.py:29
  56.1 0.0 copy-done
  56.1 5.5 %convolution_convert_fusion = bf16[12288,192]{0,1:T(8,128)(2,1)} fusion(bf16[12288,128]{1,0:T(8,128)(2,1)} %all-gather.11.cloned.1.call-done, bf16[192,128]{1,0:T(8,128)(2,1)S(1)} %copy-done), kind=kOutput, calls=%fused_computation | convolution fusion | flops 606339072 | bytes 7913472 | tf_op jit(solution)/shard_map/dot_general | solution.py:18
  61.6 7.9 %copy.12 = bf16[12288,192]{1,0:T(8,128)(2,1)} copy(bf16[12288,192]{0,1:T(8,128)(2,1)} %convolution_convert_fusion) | data formatting | bytes 9437184
  69.6 0.0 copy-start.3
  69.6 0.0 reduce-scatter.13.cloned.1.call-update
  69.6 0.0 all-gather.5.cloned.1.call-start
  69.7 0.7 all-gather.5.cloned.1.call-update
  70.3 0.0 all-gather.7.cloned.1.call-start
  70.4 0.5 all-gather.7.cloned.1.call-update
  70.9 0.0 all-gather.9.cloned.1.call-start
  71.0 91.9 %reduce-scatter.13.cloned.1.call-done = bf16[384,192]{1,0:T(8,128)(2,1)} async-done(((bf16[12288,192]{1,0:T(8,128)(2,1)}), bf16[384,192]{1,0:T(8,128)(2,1)}) %reduce-scatter.13.cloned.1.call-update) | async-done | bytes 147472
  162.8 1.1 copy.13
  163.9 50.0 %all-gather.5.cloned.1.call-done = bf16[192,4096]{1,0:T(8,128)(2,1)} async-done(((bf16[192,128]{1,0:T(8,128)(2,1)}), bf16[192,4096]{1,0:T(8,128)(2,1)}) %all-gather.5.cloned.1.call-update) | async-done | bytes 1572880 | tf_op jit(solution)/shard_map/all_gather | solution.py:24
  213.9 45.7 %all-gather.7.cloned.1.call-done = bf16[4096,384]{1,0:T(8,128)(2,1)} async-done(((bf16[512,384]{1,0:T(8,128)(2,1)}), bf16[4096,384]{1,0:T(8,128)(2,1)}) %all-gather.7.cloned.1.call-update) | async-done | bytes 3145744 | tf_op jit(solution)/shard_map/all_gather | solution.py:25
  259.6 0.0 copy-done.3
  259.6 4.2 convert_reduce_fusion
  263.8 0.0 all-gather.9.cloned.1.call-update
  263.8 0.0 reduce-scatter.15.cloned.1.call-start
  263.9 3.1 fusion.1
  267.0 0.0 copy-start.2
  267.0 2.5 copy.14
  269.5 0.0 reduce-scatter.15.cloned.1.call-update
  269.5 0.0 reduce-scatter.9.cloned.1.call-start
  269.6 0.0 copy-done.2
  269.6 2.8 fusion
  272.4 0.0 reduce-scatter.9.cloned.1.call-update
  272.4 0.0 reduce-scatter.11.cloned.1.call-start
  272.5 46.2 %all-gather.9.cloned.1.call-done = bf16[192,12288]{1,0:T(8,128)(2,1)} async-done(((bf16[192,384]{1,0:T(8,128)(2,1)}), bf16[192,12288]{1,0:T(8,128)(2,1)}) %all-gather.9.cloned.1.call-update) | async-done | bytes 4718608 | tf_op jit(solution)/shard_map/all_gather | solution.py:28
  318.7 5.9 %convolution_convert_fusion.1 = bf16[12288,128]{1,0:T(8,128)(2,1)} fusion(bf16[192,12288]{1,0:T(8,128)(2,1)} %all-gather.9.cloned.1.call-done, bf16[192,128]{1,0:T(8,128)(2,1)S(1)} %copy-done), kind=kOutput, calls=%fused_computation.1 | convolution fusion | flops 605552640 | bytes 7913472 | tf_op jit(solution)/shard_map/dot_general | solution.py:12
  324.5 0.0 copy-start.1
  324.5 0.0 reduce-scatter.11.cloned.1.call-update
  324.6 16.5 %psum.7 = f32[384]{0:T(512)} all-reduce(f32[384]{0:T(512)S(1)} %get-tuple-element.15), channel_id=1, replica_groups=mesh['row'=8,'col'=32] {'row'}, use_global_device_ids=true, to_apply=%region_4.0 | all-reduce | flops 384 | bytes 3072 | tf_op jit(solution)/shard_map/psum | solution.py:43
  341.1 67.8 %reduce-scatter.15.cloned.1.call-done = bf16[128,192]{1,0:T(8,128)(2,1)} async-done(((bf16[4096,192]{1,0:T(8,128)(2,1)}), bf16[128,192]{1,0:T(8,128)(2,1)}) %reduce-scatter.15.cloned.1.call-update) | async-done | bytes 49168
  409.0 1.6 copy.15
  410.5 46.7 %reduce-scatter.9.cloned.1.call-done = bf16[512,384]{0,1:T(8,128)(2,1)} async-done(((bf16[4096,384]{0,1:T(8,128)(2,1)}), bf16[512,384]{0,1:T(8,128)(2,1)}) %reduce-scatter.9.cloned.1.call-update) | async-done | bytes 393232 | tf_op jit(solution)/shard_map/reduce_scatter | solution.py:45
  457.3 2.0 copy.11
  459.3 0.0 copy-done.1
  459.3 4.3 convolution_convert_fusion.4
  463.6 42.6 %reduce-scatter.11.cloned.1.call-done = bf16[1536,128]{1,0:T(8,128)(2,1)} async-done(((bf16[12288,128]{1,0:T(8,128)(2,1)}), bf16[1536,128]{1,0:T(8,128)(2,1)}) %reduce-scatter.11.cloned.1.call-update) | async-done | bytes 393232 | tf_op jit(solution)/shard_map/reduce_scatter | solution.py:49
  506.2 1.9 convert_element_type.54
Async XLA Ops:
  7.2 49.0 %copy-start = (bf16[192,128]{1,0:T(8,128)(2,1)S(1)}, bf16[192,128]{1,0:T(8,128)(2,1)}, u32[]{:S(2)}) copy-start(bf16[192,128]{1,0:T(8,128)(2,1)} %param.9) | copy-start | bytes 147460
  7.2 48.9 %all-gather.11.cloned.1.call-start = ((), (), s32[]{:S(2)}) async-start(), calls=%async_computation.7 | async-start | bytes 3538944 | tf_op jit(solution)/shard_map/all_gather | solution.py:29
  7.9 154.9 %reduce-scatter.13.cloned.1.call-start = ((), (), s32[]{:S(2)}) async-start(), calls=%async_computation.10 | async-start | bytes 6488064
  69.6 190.0 %copy-start.3 = (f32[384]{0:T(512)S(1)}, f32[384]{0:T(512)}, u32[]{:S(2)}) copy-start(f32[384]{0:T(512)} %param.7) | copy-start | bytes 4612
  69.6 144.3 %all-gather.5.cloned.1.call-start = ((), (), s32[]{:S(2)}) async-start(), calls=%async_computation.4 | async-start | bytes 1622016 | tf_op jit(solution)/shard_map/all_gather | solution.py:24
  70.3 189.2 %all-gather.7.cloned.1.call-start = ((), (), s32[]{:S(2)}) async-start(), calls=%async_computation.5 | async-start | bytes 3538944 | tf_op jit(solution)/shard_map/all_gather | solution.py:25
  70.9 247.8 %all-gather.9.cloned.1.call-start = ((), (), s32[]{:S(2)}) async-start(), calls=%async_computation.6 | async-start | bytes 4866048 | tf_op jit(solution)/shard_map/all_gather | solution.py:28
  263.8 145.1 %reduce-scatter.15.cloned.1.call-start = ((), (), s32[]{:S(2)}) async-start(), calls=%async_computation.11 | async-start | bytes 2162688
  267.0 2.6 copy-start.2
  269.5 187.7 %reduce-scatter.9.cloned.1.call-start = ((), (), s32[]{:S(2)}) async-start(), calls=%async_computation.8 | async-start | bytes 3538944 | tf_op jit(solution)/shard_map/reduce_scatter | solution.py:45
  272.4 233.8 %reduce-scatter.11.cloned.1.call-start = ((), (), s32[]{:S(2)}) async-start(), calls=%async_computation.9 | async-start | bytes 3538944 | tf_op jit(solution)/shard_map/reduce_scatter | solution.py:49
  324.5 134.8 %copy-start.1 = (bf16[12288,128]{1,0:T(8,128)(2,1)S(1)}, bf16[12288,128]{1,0:T(8,128)(2,1)}, u32[]{:S(2)}) copy-start(bf16[12288,128]{1,0:T(8,128)(2,1)} %all-gather.11.cloned.1.call-done) | copy-start | bytes 9437188
Sparse Core Ops, SparseCore 0:
  9.8 46.2 all-gather.10
  69.7 93.0 reduce-scatter.12
  165.6 48.2 all-gather.4
  215.7 43.8 all-gather.6
  263.9 54.6 all-gather.8
  322.9 86.0 reduce-scatter.14
  411.7 45.5 reduce-scatter.8
  460.0 46.1 reduce-scatter.10
where the time goes:
time: 517 us; the launch traced here: 515 us
  waiting for transfers between devices  441 us (85%)
  matrix products  25.8 us (5%)
  blocking collectives  16.5 us (3%)
  local copies, waits for them, and re-layouts  15.1 us (3%)
  between operations  14.2 us (3%)
    unnamed x10, waiting for transfers between devices  162 us
    all_gather x1, waiting for transfers between devices, per_device(): all_features = lax.all_gather(tokens, 'col', axis=1, tiled=True)  50 us
    all_gather x1, waiting for transfers between devices, per_device(): out_columns = lax.all_gather(w_out, 'row', axis=0, tiled=True)  48.2 us
    reduce_scatter x1, waiting for transfers between devices, per_device(): lax.psum_scatter(contract_rows(window, grad_pre).astype(jnp.bfloat16), 'r...  46.7 us
    all_gather x1, waiting for transfers between devices, per_device(): all_hidden = lax.all_gather(hidden, 'col', axis=1, tiled=True)  46.2 us
    all_gather x1, waiting for transfers between devices, per_device(): in_columns = lax.all_gather(w_in, 'row', axis=0, tiled=True)  45.7 us
    reduce_scatter x1, waiting for transfers between devices, per_device(): lax.psum_scatter(contract_rows(window, grad_out).astype(jnp.bfloat16), 'r...  42.6 us
    psum x1, blocking collectives, per_device(): grad_bias = lax.psum(jnp.sum(grad_pre, axis=0, dtype=jnp.float32), 'row')  16.5 us
  transfers between devices with their start and end apart: 8, of which 8 were waited for; matrix products, arithmetic and copies ran while one was open for 5% of the time, Pallas kernels for 0%

commit v1 on v0

v1 whole, which is shorter than its diff:
```python
import functools

import jax
import jax.numpy as jnp
from jax import lax
from jax.experimental import pallas as pl
from jax.experimental.pallas import tpu as pltpu
from jax.sharding import PartitionSpec as P

MESH = pl.DeviceIdType.MESH
BF, F32 = jnp.bfloat16, jnp.float32
S2PI = 0.7978845608028654
CUBIC = 0.044715


def dot(a, b):
    return lax.dot_general(a, b, (((1,), (0,)), ((), ())), preferred_element_type=F32)


def dot_t(a, b):
    return lax.dot_general(a, b, (((1,), (1,)), ((), ())), preferred_element_type=F32)


def t_dot(a, b):
    return lax.dot_general(a, b, (((0,), (0,)), ((), ())), preferred_element_type=F32)


def col(y, x, k):
    return y * 8 + x * 2 + k


def lanes(i, n):
    return pl.ds(pl.multiple_of(i * n, n), n)


def kernel(
    tok, w1, bias, w2, go,
    out_y, out_x, out_w1, out_b, out_w2,
    xa, xg, w1g, w2g, gs, gg, b8, bg,
    ps, pr, dhs, dhr, ho, dpo, hg, dpg,
    ys, ya, yb, yr, d2s, d2r, dxs, dxr, dxb, ot, d1s, d1r, bs, dbr,
    send, x1_r, x2_r, w1_r, w2_r, b_r, g1_r, g2_r, g3_r, p_r, dh_r, h_r, dp_r,
    y1_r, y2_r, d2_r, dx1_r, dx2_r, d1_r, db_r,
):
    z, c = lax.axis_index("row"), lax.axis_index("col")
    k, x, y = c % 2, (c // 2) % 4, c // 8
    sent = []

    def put(src, dst, rsem, dev):
        i = len(sent)
        copy = pltpu.make_async_remote_copy(
            src_ref=src, dst_ref=dst, send_sem=send.at[i], recv_sem=rsem,
            device_id=dev, device_id_type=MESH,
        )
        copy.start()
        sent.append((copy, None))

    def put_if(cond, src, dst, rsem, dev):
        i = len(sent)
        copy = pltpu.make_async_remote_copy(
            src_ref=src, dst_ref=dst, send_sem=send.at[i], recv_sem=rsem,
            device_id=dev, device_id_type=MESH,
        )
        pl.when(cond)(copy.start)
        sent.append((copy, cond))

    def put_any(src, dst, rsem, dev, here):
        put_if(jnp.logical_not(here), src, dst, rsem, dev)
        pl.when(here)(pltpu.make_async_copy(src, dst, rsem).start)

    def keep(src, dst, rsem):
        pltpu.make_async_copy(src, dst, rsem).start()

    def got(dst, rsem):
        pltpu.make_async_copy(dst, dst, rsem).wait()

    barrier = pltpu.get_barrier_semaphore()
    near = [((z + i) % 8, c) for i in range(1, 8)]
    near += [(z, col((y + i) % 4, x, (k + d) % 2)) for i in range(4) for d in range(2) if i or d]
    near += [(z, col(y, (x + i) % 4, (k + d) % 2)) for i in range(1, 4) for d in range(2)]
    far = [(2 * y + x // 2, col(z // 2, j, x % 2)) for j in range(4)]
    back = [(2 * y + h, col(z // 2, 2 * (z % 2) + k, d)) for h in range(2) for d in range(2)]
    for dev in near + far + back:
        pl.semaphore_signal(barrier, inc=1, device_id=dev, device_id_type=MESH)
    pl.semaphore_wait(barrier, len(near + far + back))

    for j in range(4):
        here = jnp.logical_and(far[j][0] == z, far[j][1] == c)
        put_any(
            tok.at[pl.ds(j * 48, 48)], xa.at[z % 2, :, lanes(k, 128)], x1_r.at[z % 2, k], far[j], here
        )
    at_row = y == z // 2
    put_any(go, gs.at[:, lanes(y, 128)], g1_r.at[y], (z, col(z // 2, x, k)), at_row)
    b8[...] = jnp.broadcast_to(bias[...], b8.shape)
    keep(w1, w1g.at[y], w1_r.at[y])
    keep(b8, bg.at[y], b_r.at[y])
    half = [w2.at[lanes((k + d) % 2, 768)] for d in range(2)]
    keep(half[0], w2g.at[k, :, lanes(y, 128)], w2_r.at[y, k])
    put(half[1], w2g.at[k, :, lanes(y, 128)], w2_r.at[y, k], (z, col(y, x, 1 - k)))
    for i in (1, 3, 2):
        put(w1, w1g.at[y], w1_r.at[y], (z, col((y + i) % 4, x, k)))
        put(b8, bg.at[y], b_r.at[y], (z, col((y + i) % 4, x, k)))
    for i in (1, 3, 2):
        for d in range(2):
            put(
                half[d], w2g.at[k, :, lanes(y, 128)], w2_r.at[y, k],
                (z, col((y + i) % 4, x, (k + d) % 2)),
            )

    for h in range(2):
        for d in range(2):
            got(xa.at[h, :, pl.ds(d * 128, 128)], x1_r.at[h, d])
    keep(xa, xg.at[k, :, x], x2_r.at[x, k])
    for i in range(4):
        for d in range(2):
            if i or d:
                put(xa, xg.at[k, :, x], x2_r.at[x, k], (z, col(y, (x + i) % 4, (k + d) % 2)))

    @pl.when(at_row)
    def _():
        for i in range(4):
            got(gs.at[:, pl.ds(i * 128, 128)], g1_r.at[i])
        keep(gs, gg.at[k, z % 2], g2_r.at[z % 2])

    for i in (4, 3, 5, 2, 6, 1, 7):
        put_if(at_row, gs, gg.at[k, z % 2], g2_r.at[z % 2], ((z + i) % 8, c))

    for i in range(4):
        for d in range(2):
            got(xg.at[d, :, i], x2_r.at[i, d])
    for i in range(4):
        got(w1g.at[i], w1_r.at[i])

    def part(i, _):
        x0 = xg[0].reshape(384, 256)
        x1 = xg[1].reshape(384, 256)
        ps[i] = (dot(x0, w1g[i, :256]) + dot(x1, w1g[i, 256:])).astype(BF)
        return 0

    owner = z % 2 == x // 2
    lax.fori_loop(0, 4, part, 0)
    for i in range(4):
        dest = 2 * i + x // 2
        put_any(ps.at[i], pr.at[z], p_r.at[z], (dest, c), dest == z)

    for h in range(2):
        got(gg.at[k, h], g2_r.at[h])
    put(gg.at[k], gg.at[k], g3_r, (z, col(y, x, 1 - k)))
    got(gg.at[1 - k], g3_r)
    for i in range(4):
        for d in range(2):
            got(w2g.at[d, :, pl.ds(i * 128, 128)], w2_r.at[i, d])

    def part_hidden(i, _):
        rows = pl.ds(pl.multiple_of(i * 384, 384), 384)
        g0 = gg[0].reshape(384, 512)
        g1 = gg[1].reshape(384, 512)
        dhs[i] = (dot_t(g0, w2g[0, rows, :]) + dot_t(g1, w2g[1, rows, :])).astype(BF)
        return 0

    lax.fori_loop(0, 2, part_hidden, 0)
    home = 2 * (z % 2) + k
    for i in range(2):
        put_any(
            dhs.at[i], dhr.at[x], dh_r.at[x], (z, col(y, home, i)),
            jnp.logical_and(home == x, k == i),
        )

    @pl.when(owner)
    def _():
        for i in range(4):
            got(bg.at[i], b_r.at[i])
        for i in range(8):
            got(pr.at[i], p_r.at[i])
        for i in range(4):
            got(dhr.at[i], dh_r.at[i])

        def point(i, _):
            rows = pl.ds(pl.multiple_of(i * 16, 16), 16)
            v = jnp.broadcast_to(bg[z // 2, pl.ds(0, 1), :], (16, 384))
            for j in range(8):
                v = v + pr[j, rows, :].astype(F32)
            up = dhr[0, rows, :].astype(F32)
            for j in range(1, 4):
                up = up + dhr[j, rows, :].astype(F32)
            v2 = v * v
            t = jnp.tanh(S2PI * (v + CUBIC * (v2 * v)))
            cdf = 0.5 * (1.0 + t)
            ho[rows, :] = (v * cdf).astype(BF)
            slope = cdf + (0.5 * v) * (1.0 - t * t) * (S2PI * (1.0 + 3.0 * CUBIC * v2))
            dpo[rows, :] = (up * slope).astype(BF)
            return 0

        lax.fori_loop(0, 24, point, 0)
        keep(dpo, dpg.at[z // 2], dp_r.at[z // 2])

    @pl.when(jnp.logical_not(owner))
    def _():
        for i in range(4):
            got(bg.at[i], b_r.at[i])

    for i in range(4):
        put_any_if = jnp.logical_and((x + i) % 4 == x, x % 2 == k)
        dev = (z, col(y, (x + i) % 4, x % 2))
        put_if(jnp.logical_and(owner, jnp.logical_not(put_any_if)), ho, hg.at[k], h_r.at[k], dev)
        pl.when(jnp.logical_and(owner, put_any_if))(
            pltpu.make_async_copy(ho, hg.at[k], h_r.at[k]).start
        )
    for i in (4, 3, 5, 2, 6, 1, 7):
        put_if(owner, dpo, dpg.at[z // 2], dp_r.at[z // 2], ((z + i) % 8, c))

    for i in range(2):
        got(hg.at[i], h_r.at[i])

    def part_out(i, _):
        o = dot(hg[0], w2g[i, :384, :]) + dot(hg[1], w2g[i, 384:, :])
        for j in range(4):
            ys[i, j] = o[:, j * 128:(j + 1) * 128].astype(BF)
        return 0

    lax.fori_loop(0, 2, part_out, 0)
    for i in range(4):
        for d in range(2):
            dy, dk = (y + i) % 4, (k + d) % 2
            if i or d:
                put(ys.at[dk, dy], ya.at[y, k], y1_r.at[y, k], (z, col(dy, x, dk)))
            else:
                keep(ys.at[dk, dy], ya.at[y, k], y1_r.at[y, k])

    def part_w2(i, _):
        g = gg[i].reshape(384, 512)
        for r in range(2):
            o = t_dot(hg[r], g)
            for j in range(4):
                d2s[i, j, pl.ds(r * 384, 384), :] = o[:, j * 128:(j + 1) * 128].astype(BF)
        return 0

    lax.fori_loop(0, 2, part_w2, 0)
    for i in (0, 1, 3, 2):
        for d in range(2):
            dy, dk = (y + i) % 4, (k + d) % 2
            if i or d:
                put(d2s.at[dk, dy], d2r.at[y, k], d2_r.at[y, k], (z, col(dy, x, dk)))
            else:
                keep(d2s.at[dk, dy], d2r.at[y, k], d2_r.at[y, k])

    for i in range(4):
        got(dpg.at[i], dp_r.at[i])
    for i in range(2):
        o = dot_t(dpg[0], w1g[0, pl.ds(i * 256, 256), :])
        for j in range(1, 4):
            o = o + dot_t(dpg[j], w1g[j, pl.ds(i * 256, 256), :])
        dxs[i] = o.astype(BF).reshape(2, 4, 48, 256)
    for i in range(4):
        for d in range(2):
            dx, dk = (x + i) % 4, (k + d) % 2
            if i or d:
                put(dxs.at[dk, :, dx], dxr.at[x, k], dx1_r.at[x, k], (z, col(y, dx, dk)))
            else:
                keep(dxs.at[dk, :, dx], dxr.at[x, k], dx1_r.at[x, k])

    def part_w1(i, _):
        for r in range(2):
            d1s[i, pl.ds(r * 256, 256), :] = t_dot(xg[r].reshape(384, 256), dpg[i]).astype(BF)
        total = jnp.sum(dpg[i].astype(F32), axis=0, keepdims=True)
        bs[i] = jnp.broadcast_to(total, (8, 384))
        return 0

    lax.fori_loop(0, 4, part_w1, 0)
    keep(d1s.at[y], d1r.at[y], d1_r.at[y])
    keep(bs.at[y], dbr.at[y], db_r.at[y])
    for i in (1, 3, 2):
        dy = (y + i) % 4
        put(d1s.at[dy], d1r.at[y], d1_r.at[y], (z, col(dy, x, k)))
        put(bs.at[dy], dbr.at[y], db_r.at[y], (z, col(dy, x, k)))

    for i in range(4):
        for d in range(2):
            got(ya.at[i, d], y1_r.at[i, d])
    for i in range(8):
        rows = pl.ds((i % 2) * 192, 192)
        yb[i] = (ya[i // 2, 0, rows, :].astype(F32) + ya[i // 2, 1, rows, :].astype(F32)).astype(BF)
    for i in range(8):
        j = (z + i) % 8
        if i:
            put(yb.at[j], yr.at[z], y2_r.at[z], (j, c))
        else:
            keep(yb.at[j], yr.at[z], y2_r.at[z])

    for i in range(4):
        for d in range(2):
            got(dxr.at[i, d], dx1_r.at[i, d])
    for h in range(2):
        o = dxr[0, 0, h].astype(F32)
        for j in range(1, 8):
            o = o + dxr[j // 2, j % 2, h].astype(F32)
        for d in range(2):
            dxb[h, d] = o[:, d * 128:(d + 1) * 128].astype(BF)
    for h in range(2):
        for d in range(2):
            dev = back[2 * h + d]
            put_any(
                dxb.at[h, d], ot.at[x], dx2_r.at[x], dev,
                jnp.logical_and(dev[0] == z, dev[1] == c),
            )

    for i in range(4):
        for d in range(2):
            got(d2r.at[i, d], d2_r.at[i, d])

    def sum_w2(i, _):
        for d in range(2):
            rows = pl.ds(pl.multiple_of(i * 64, 64), 64)
            o = d2r[0, d, rows, :].astype(F32)
            for j in range(1, 4):
                o = o + d2r[j, d, rows, :].astype(F32)
            out_w2[pl.ds(pl.multiple_of(d * 768 + i * 64, 64), 64), :] = o
        return 0

    lax.fori_loop(0, 12, sum_w2, 0)
    for i in range(8):
        got(yr.at[i], y2_r.at[i])
    o = yr[0].astype(F32)
    for j in range(1, 8):
        o = o + yr[j].astype(F32)
    out_y[...] = o.astype(BF)
    for i in range(4):
        got(ot.at[i], dx2_r.at[i])
    out_x[...] = ot[...].reshape(192, 128)
    for i in range(4):
        got(d1r.at[i], d1_r.at[i])
        got(dbr.at[i], db_r.at[i])

    def sum_w1(i, _):
        rows = pl.ds(pl.multiple_of(i * 32, 32), 32)
        o = d1r[0, rows, :].astype(F32)
        for j in range(1, 4):
            o = o + d1r[j, rows, :].astype(F32)
        out_w1[rows, :] = o
        return 0

    lax.fori_loop(0, 16, sum_w1, 0)
    o = dbr[0] + dbr[1] + dbr[2] + dbr[3]
    out_b[...] = o[:1]

    for copy, cond in sent:
        if cond is None:
            copy.wait_send()
        else:
            pl.when(cond)(copy.wait_send)


SENDS = 160
DMA = pltpu.SemaphoreType.DMA


def per_device(tokens, w_in, bias_in, w_out, grad_out):
    vm = pltpu.VMEM
    spec = pl.BlockSpec(memory_space=pltpu.VMEM)
    shapes = [
        ((192, 128), BF), ((192, 128), BF), ((512, 384), F32), ((1, 384), F32), ((1536, 128), F32),
    ]
    out = pl.pallas_call(
        kernel,
        out_shape=[jax.ShapeDtypeStruct(s, d) for s, d in shapes],
        in_specs=[spec] * 5,
        out_specs=[spec] * 5,
        scratch_shapes=[
            vm((2, 48, 256), BF),
            vm((2, 2, 4, 48, 256), BF),
            vm((4, 512, 384), BF),
            vm((2, 768, 512), BF),
            vm((192, 512), BF),
            vm((2, 2, 192, 512), BF),
            vm((8, 384), F32),
            vm((4, 8, 384), F32),
            vm((4, 384, 384), BF),
            vm((8, 384, 384), BF),
            vm((2, 384, 384), BF),
            vm((4, 384, 384), BF),
            vm((384, 384), BF),
            vm((384, 384), BF),
            vm((2, 384, 384), BF),
            vm((4, 384, 384), BF),
            vm((2, 4, 384, 128), BF),
            vm((4, 2, 384, 128), BF),
            vm((8, 192, 128), BF),
            vm((8, 192, 128), BF),
            vm((2, 4, 768, 128), BF),
            vm((4, 2, 768, 128), BF),
            vm((2, 2, 4, 48, 256), BF),
            vm((4, 2, 2, 48, 256), BF),
            vm((2, 2, 48, 128), BF),
            vm((4, 48, 128), BF),
            vm((4, 512, 384), BF),
            vm((4, 512, 384), BF),
            vm((4, 8, 384), F32),
            vm((4, 8, 384), F32),
            DMA((SENDS,)),
            DMA((2, 2)), DMA((4, 2)), DMA((4,)), DMA((4, 2)), DMA((4,)),
            DMA((4,)), DMA((2,)), DMA, DMA((8,)), DMA((4,)), DMA((2,)), DMA((4,)),
            DMA((4, 2)), DMA((8,)), DMA((4, 2)), DMA((4, 2)), DMA((4,)), DMA((4,)), DMA((4,)),
        ],
        compiler_params=pltpu.CompilerParams(
            collective_id=0, has_side_effects=True, vmem_limit_bytes=56 * 2**20
        ),
        name="mlp_grad",
    )(tokens, w_in, bias_in.reshape(1, 384), w_out, grad_out)
    block_out, grad_tokens, grad_w_in, grad_bias, grad_w_out = out
    return block_out, grad_tokens, grad_w_in, grad_bias.reshape(384), grad_w_out


def solution(mesh):
    return jax.shard_map(
        per_device,
        mesh=mesh,
        in_specs=(P("row", "col"), P("row", "col"), P("col"), P("row", "col"), P("row", "col")),
        out_specs=(P("row", "col"), P("row", "col"), P("row", "col"), P("col"), P("row", "col")),
        check_vma=False,
    )
```

time: 517 us -> 171 us (0.33)
  waiting for transfers between devices: 441 us -> 0 us
  Pallas kernels: 0 us -> 162 us
  matrix products: 25.8 us -> 0 us
  blocking collectives: 16.5 us -> 0 us
  between operations: 14.2 us -> 0.65 us
  local copies, waits for them, and re-layouts: 15.1 us -> 6.97 us
    all_gather x4 -> x0, waiting for transfers between devices: 190 us -> none  [the longest x1 50 us: per_device(): all_features = lax.all_gather(tokens, 'col', axis=1, tiled=True)]
    pallas_call x0 -> x1, Pallas kernels: none -> 162 us  [per_device(): pl.pallas_call(kernel, out_shape=[jax.ShapeDtypeStruct(s, d) for s, d in...]
    unnamed x10 -> x0, waiting for transfers between devices: 162 us -> none
    reduce_scatter x2 -> x0, waiting for transfers between devices: 89.3 us -> none  [the longest x1 46.7 us: per_device(): lax.psum_scatter(contract_rows(window, grad_pre).astype(jnp.bfloat16), 'r...]
    dot_general x6 -> x0, matrix products: 25.8 us -> none  [the longest x2 8.64 us: contract_cols(): lax.dot_general(left, right, (((1,), (1,)), ((), ())), preferred_element_...]
    psum x1 -> x0, blocking collectives: 16.5 us -> none  [per_device(): grad_bias = lax.psum(jnp.sum(grad_pre, axis=0, dtype=jnp.float32), 'row')]
    unnamed x13 -> x10, local copies, waits for them, and re-layouts: 15.1 us -> 5.73 us
  transfers between devices with their start and end apart: 8 -> 0, of which waited for: 8 -> 0; matrix products, arithmetic and copies ran while one was open for 5% -> 0% of each run, Pallas kernels for 0% -> 0%
where the time goes in v1:
time: 171 us; the launch traced here: 170 us
  Pallas kernels  162 us (95%)
  local copies, waits for them, and re-layouts  6.97 us (4%)
    pallas_call x1, Pallas kernels, per_device(): pl.pallas_call(kernel, out_shape=[jax.ShapeDtypeStruct(s, d) for s, d in...  162 us
    unnamed x10, local copies, waits for them, and re-layouts  5.73 us

profile of v1, /device:TPU:96, one launch (start us, length us, event | category | flops | bytes accessed | tf_op | source)
XLA Modules:
  0.0 170.4 jit_solution(16196165390750402434)
XLA Ops:
  0.6 1.2 reshape.16.bias
  1.9 162.2 %mlp_grad.1 = (bf16[192,128]{1,0:T(8,128)(2,1)}, bf16[192,128]{1,0:T(8,128)(2,1)}, f32[512,384]{1,0:T(8,128)}, f32[1,384]{1,0:T(1,128)}, f32[1536,128]{1,0:T(8,128)}) custom-call(bf16[192,128]{1,0:T(8,128)(2,1)} %tok.1, bf16[512,384]{1,0:T(8,128)(2,1)} %w1.1, f32[1,384]{1,0:T(1,128)} %reshape.16.bias, bf16[1536,128]{1,0:T(8,128)(2,1)} %w2.1, bf16[192,128]{1,0:T(8,128)(2,1)} %go.1), custom_call_target="tpu_custom_call" | custom-call | tf_op jit(solution)/shard_map/mlp_grad/pallas_call | solution.py:363
  164.1 0.0 copy-start.2
  164.1 0.7 copy-done.2
  164.8 0.6 reduce
  165.4 0.0 copy-start.1
  165.4 1.4 copy.14
  166.8 0.0 copy-done.1
  166.8 0.6 copy.15
  167.4 0.0 copy-start
  167.4 2.1 %copy.16 = f32[512,384]{1,0:T(8,128)} copy(f32[512,384]{1,0:T(8,128)} %get-tuple-element.22) | data formatting | bytes 1572864
  169.6 0.0 copy-done
  169.6 0.9 copy.17
Async XLA Ops:
  164.1 0.7 copy-start.2
  165.4 1.4 copy-start.1
  167.4 2.1 %copy-start = (f32[1536,128]{1,0:T(8,128)S(1)}, f32[1536,128]{1,0:T(8,128)}, u32[]{:S(2)}) copy-start(f32[1536,128]{1,0:T(8,128)} %get-tuple-element.24) | copy-start | bytes 2359300

commit v2 on v1

v2 whole, which is shorter than its diff:
```python
import functools

import jax
import jax.numpy as jnp
from jax import lax
from jax.experimental import pallas as pl
from jax.experimental.pallas import tpu as pltpu
from jax.sharding import PartitionSpec as P

MESH = pl.DeviceIdType.MESH
BF, F32 = jnp.bfloat16, jnp.float32
S2PI = 0.7978845608028654
CUBIC = 0.044715


def dot(a, b):
    return lax.dot_general(a, b, (((1,), (0,)), ((), ())), preferred_element_type=F32)


def dot_t(a, b):
    return lax.dot_general(a, b, (((1,), (1,)), ((), ())), preferred_element_type=F32)


def t_dot(a, b):
    return lax.dot_general(a, b, (((0,), (0,)), ((), ())), preferred_element_type=F32)


def col(y, x, k):
    return y * 8 + x * 2 + k


def lanes(i, n):
    return pl.ds(pl.multiple_of(i * n, n), n)


def kernel(
    tok, w1, bias, w2, go,
    out_y, out_x, out_w1, out_b, out_w2,
    xa, xg, w1g, w2h, w2g, gs, gg, b8, bg,
    ps, rz, tz, dhs, dhr, ho, hg, dpg,
    ys, yx, ya, yr, d2s, d2x, d2t, d2r, dxs, dxr, dxb, ot, d1s, d1t, d1r, bs, dbr,
    send, x1_r, x2_r, w1_r, w2s_r, w2k_r, w2_r, b_r, g1_r, g2_r, g3_r, p_r, dh_r, h_r, dp_r,
    yx_r, y1_r, y2_r, d2x_r, d2t_r, d2_r, dx1_r, dx2_r, d1t_r, d1_r, db_r,
):
    z, c = lax.axis_index("row"), lax.axis_index("col")
    k, x, y = c % 2, (c // 2) % 4, c // 8
    sent = []

    def put(src, dst, rsem, dev, cond=None, like=None):
        copy = pltpu.make_async_remote_copy(
            src_ref=src, dst_ref=dst, send_sem=send.at[len(sent)], recv_sem=rsem,
            device_id=dev, device_id_type=MESH,
        )
        if cond is None or like is not None:
            copy.start()
        else:
            pl.when(cond)(copy.start)
        sent.append((like or (lambda: src), cond))

    def put_any(src, dst, rsem, dev, here):
        put(src, dst, rsem, dev, jnp.logical_not(here))
        pl.when(here)(pltpu.make_async_copy(src, dst, rsem).start)

    def keep(src, dst, rsem):
        pltpu.make_async_copy(src, dst, rsem).start()

    def got(dst, rsem):
        pltpu.make_async_copy(dst, dst, rsem).wait()

    barrier = pltpu.get_barrier_semaphore()
    near = [((z + i) % 8, c) for i in range(1, 8)]
    near += [(z, col((y + i) % 4, x, (k + d) % 2)) for i in range(4) for d in range(2) if i or d]
    near += [(z, col(y, (x + i) % 4, (k + d) % 2)) for i in range(1, 4) for d in range(2)]
    far = [(2 * y + x // 2, col(z // 2, j, x % 2)) for j in range(4)]
    back = [(2 * y + h, col(z // 2, 2 * (z % 2) + k, d)) for h in range(2) for d in range(2)]
    for dev in near + far + back:
        pl.semaphore_signal(barrier, inc=1, device_id=dev, device_id_type=MESH)
    pl.semaphore_wait(barrier, len(near + far + back))

    for j in range(4):
        here = jnp.logical_and(far[j][0] == z, far[j][1] == c)
        put_any(
            tok.at[pl.ds(j * 48, 48)], xa.at[z % 2, :, lanes(k, 128)], x1_r.at[z % 2, k], far[j], here
        )
    keep(go, gs.at[z], g1_r.at[z])
    for i in (4, 3, 5, 2, 6, 1, 7):
        put(go, gs.at[z], g1_r.at[z], ((z + i) % 8, c))
    up, down = (y + 1) % 4, (y + 3) % 4
    b8[...] = jnp.broadcast_to(bias[...], b8.shape)
    for i in range(2):
        rows = pl.ds(i * 256, 256)
        keep(w1.at[rows], w1g.at[y, rows], w1_r.at[y, i])
    for i in range(2):
        for n, dy in enumerate((up, down)):
            rows = pl.ds((i ^ n) * 256, 256)
            put(w1.at[rows], w1g.at[y, rows], w1_r.at[y, i ^ n], (z, col(dy, x, k)))
    mine = pl.ds(pl.multiple_of(k * 768, 768), 768)
    theirs = pl.ds(pl.multiple_of((1 - k) * 768, 768), 768)
    put(w2.at[theirs], w2h, w2s_r, (z, col(y, x, 1 - k)))
    keep(w2.at[mine], w2g.at[k, :, lanes(y, 128)], w2k_r)
    keep(b8, bg.at[y], b_r.at[y])
    for i in (1, 2, 3):
        put(b8, bg.at[y], b_r.at[y], (z, col((y + i) % 4, x, k)))
    for h in range(2):
        for d in range(2):
            got(xa.at[h, :, pl.ds(d * 128, 128)], x1_r.at[h, d])
    keep(xa, xg.at[k, :, x], x2_r.at[x, k])
    for i in range(4):
        for d in range(2):
            if i or d:
                put(xa, xg.at[k, :, x], x2_r.at[x, k], (z, col(y, (x + i) % 4, (k + d) % 2)))

    for i, (dy, fy) in enumerate(((up, down), (down, up))):
        rows = pl.ds(i * 256, 256)
        got(w1g.at[fy, rows], w1_r.at[fy, i])
        put(w1g.at[fy, rows], w1g.at[fy, rows], w1_r.at[fy, i], (z, col(dy, x, k)))
    got(w2h, w2s_r)
    keep(w2h, w2g.at[1 - k, :, lanes(y, 128)], w2s_r)
    for i in range(2):
        for dy in (up, down):
            rows = pl.ds(pl.multiple_of(k * 768 + i * 384, 384), 384)
            put(
                w2.at[rows], w2g.at[k, pl.ds(i * 384, 384), lanes(y, 128)], w2_r.at[y, k, i],
                (z, col(dy, x, k)),
            )
            rows = pl.ds(i * 384, 384)
            put(
                w2h.at[rows], w2g.at[1 - k, rows, lanes(y, 128)], w2_r.at[y, 1 - k, i],
                (z, col(dy, x, k)),
            )

    def pass_w2(i):
        for d, (dy, fy) in enumerate(((up, down), (down, up))):
            block = w2g.at[d, pl.ds(i * 384, 384), lanes(fy, 128)]
            got(block, w2_r.at[fy, d, i])
            put(block, block, w2_r.at[fy, d, i], (z, col(dy, x, k)))

    for i in range(8):
        got(gs.at[i], g1_r.at[i])
    for i in (2, 1, 3, 0):
        dy = (y + i) % 4
        src, dst = gs.at[pl.ds(2 * dy, 2)], gg.at[k, :, :, lanes(y, 128)]
        if i:
            put(src, dst, g2_r.at[y], (z, col(dy, x, k)))
        else:
            keep(src, dst, g2_r.at[y])

    for i in range(4):
        for d in range(2):
            got(xg.at[d, :, i], x2_r.at[i, d])
    got(w1g.at[y, pl.ds(0, 256)], w1_r.at[y, 0])
    got(w1g.at[y, pl.ds(256, 256)], w1_r.at[y, 1])
    got(w1g.at[down, pl.ds(256, 256)], w1_r.at[down, 1])
    got(w1g.at[up, pl.ds(0, 256)], w1_r.at[up, 0])
    for i in range(2):
        got(w1g.at[(y + 2) % 4, pl.ds(i * 256, 256)], w1_r.at[(y + 2) % 4, i])

    owner = z % 2 == x // 2
    other = jnp.logical_not(owner)
    odd = (z + x // 2) % 2
    ways = ((1, 0), (-1, 1))
    ahead = [((z + 1) % 8, c), ((z + 7) % 8, c)]

    def block_at(step):
        return ((z + step + 16) % 8) // 2

    first = [block_at(s * (4 - odd)) for s, _ in ways]
    second = [block_at(s * (2 - odd)) for s, _ in ways]

    def piece(j):
        return pl.ds(j * 96, 96)

    def halves(q):
        return (2, 3, 0, 1) if q else (0, 1, 2, 3)

    def part(i, _):
        x0 = xg[0].reshape(384, 256)
        x1 = xg[1].reshape(384, 256)
        ps[i] = (dot(x0, w1g[i, :256]) + dot(x1, w1g[i, 256:])).astype(BF)
        return 0

    lax.fori_loop(0, 4, part, 0)
    for n in range(2):
        for _, q in ways:
            for cond, j in ((owner, halves(q)[n]), (other, halves(q)[2 + n])):
                put(
                    ps.at[first[q], piece(j)], rz.at[q, 0, piece(j)], p_r.at[q, 0, j],
                    ahead[q], cond,
                )
    home = 2 * (z % 2) + k

    def part_hidden(i):
        for d in range(2):
            for j in (down if d else up, (y + 2) % 4):
                got(w2g.at[d, pl.ds(i * 384, 384), lanes(j, 128)], w2_r.at[j, d, i])
        rows = pl.ds(i * 384, 384)
        g0 = gg[0].reshape(384, 512)
        g1 = gg[1].reshape(384, 512)
        dhs[i] = (dot_t(g0, w2g[0, rows, :]) + dot_t(g1, w2g[1, rows, :])).astype(BF)
        put_any(
            dhs.at[i], dhr.at[x], dh_r.at[x], (z, col(y, home, i)),
            jnp.logical_and(home == x, k == i),
        )

    def relay(cond, mine, kind, to, n, q):
        j = (halves(q) if kind == to == 0 else halves(1 - q))[n]
        got(rz.at[q, kind, piece(j)], p_r.at[q, kind, j])
        tz[q, to, piece(j), :] = ps[mine, piece(j), :] + rz[q, kind, piece(j), :]
        put(
            tz.at[q, to, piece(j)], rz.at[q, to, piece(j)], p_r.at[q, to, j], ahead[q], cond,
            lambda: tz.at[q, to, piece(j)],
        )

    for i in range(4):
        got(gg.at[k, :, :, pl.ds(i * 128, 128)], g2_r.at[i])
    put(gg.at[k], gg.at[k], g3_r, (z, col(y, x, 1 - k)))

    @pl.when(other)
    def _():
        for n in range(2):
            for _, q in ways:
                relay(other, first[q], 0, 0, n, q)

    got(w2g.at[k, :, lanes(y, 128)], w2k_r)
    got(w2g.at[1 - k, :, lanes(y, 128)], w2s_r)
    pass_w2(0)

    @pl.when(owner)
    def _():
        for n in range(4):
            for _, q in ways:
                relay(owner, second[q], 0, 1, n, q)

    pass_w2(1)

    got(gg.at[1 - k], g3_r)
    part_hidden(0)
    part_hidden(1)

    @pl.when(other)
    def _():
        for n in range(4):
            for _, q in ways:
                relay(other, second[q], 1, 1, n, q)

    @pl.when(owner)
    def _():
        for i in range(4):
            got(bg.at[i], b_r.at[i])
        for j in range(4):
            for _, q in ways:
                got(rz.at[q, 1, piece(j)], p_r.at[q, 1, j])
        for i in range(4):
            got(dhr.at[i], dh_r.at[i])

        def point(i, _):
            rows = pl.ds(pl.multiple_of(i * 16, 16), 16)
            v = jnp.broadcast_to(bg[z // 2, pl.ds(0, 1), :], (16, 384))
            v = v + ps[z // 2, rows, :].astype(F32)
            v = v + (rz[0, 1, rows, :].astype(F32) + rz[1, 1, rows, :].astype(F32))
            grad = dhr[0, rows, :].astype(F32)
            for j in range(1, 4):
                grad = grad + dhr[j, rows, :].astype(F32)
            v2 = v * v
            t = jnp.tanh(S2PI * (v + CUBIC * (v2 * v)))
            cdf = 0.5 * (1.0 + t)
            ho[rows, :] = (v * cdf).astype(BF)
            slope = cdf + (0.5 * v) * (1.0 - t * t) * (S2PI * (1.0 + 3.0 * CUBIC * v2))
            dpg[z // 2, rows, :] = (grad * slope).astype(BF)
            return 0

        lax.fori_loop(0, 24, point, 0)
        for n in range(4):
            for _, q in ways:
                block = dpg.at[z // 2, piece(halves(q)[n])]
                put(block, block, dp_r.at[z // 2, halves(q)[n]], ahead[q], owner, lambda: dpg.at[0, piece(0)])

    @pl.when(jnp.logical_not(owner))
    def _():
        for i in range(4):
            got(bg.at[i], b_r.at[i])

    for i in range(4):
        here = jnp.logical_and((x + i) % 4 == x, x % 2 == k)
        put(
            ho, hg.at[k], h_r.at[k], (z, col(y, (x + i) % 4, x % 2)),
            jnp.logical_and(owner, jnp.logical_not(here)),
        )
        pl.when(jnp.logical_and(owner, here))(
            pltpu.make_async_copy(ho, hg.at[k], h_r.at[k]).start
        )

    def pass_on(cond, back_by, all_rows):
        for n in range(4):
            for s, q in ways:
                j = halves(q)[n]
                block = dpg.at[block_at(-s * back_by), piece(j)]
                sem = dp_r.at[block_at(-s * back_by), j]
                got(block, sem)
                if all_rows or n < 2:
                    put(block, block, sem, ahead[q], cond, lambda: dpg.at[0, piece(0)])

    pl.when(other)(lambda: pass_on(other, 1, True))
    pl.when(owner)(lambda: pass_on(owner, 2, True))

    for i in range(2):
        got(hg.at[i], h_r.at[i])

    def part_out(i):
        o = dot(hg[0], w2g[i, :384, :]) + dot(hg[1], w2g[i, 384:, :])
        return o.astype(BF)

    o = part_out(1 - k)
    for j in range(4):
        ys[0, j] = o[:, j * 128:(j + 1) * 128]
    put(ys.at[0], yx, yx_r, (z, col(y, x, 1 - k)))
    o = part_out(k)
    for j in range(4):
        ys[1, j] = o[:, j * 128:(j + 1) * 128]
    pl.when(other)(lambda: pass_on(other, 3, False))
    got(yx, yx_r)
    for j in range(4):
        ys[1, j] = ys[1, j] + yx[j]
    keep(ys.at[1, y], ya.at[y], y1_r.at[y])
    for i in (1, 3, 2):
        put(ys.at[1, (y + i) % 4], ya.at[y], y1_r.at[y], (z, col((y + i) % 4, x, k)))

    def part_w2(i, _):
        g = gg[i].reshape(384, 512)
        for r in range(2):
            o = t_dot(hg[r], g)
            for j in range(4):
                d2s[i, j, pl.ds(r * 384, 384), :] = o[:, j * 128:(j + 1) * 128].astype(BF)
        return 0

    lax.fori_loop(0, 2, part_w2, 0)
    for i in (2, 1, 3, 0):
        j = (y + i) % 4
        put(d2s.at[1 - k, j], d2x.at[j], d2x_r.at[j], (z, col(y, x, 1 - k)))

    @pl.when(owner)
    def _():
        for j in range(4):
            got(dpg.at[block_at(4), piece(j)], dp_r.at[block_at(4), j])

    for i in range(2):
        o = dot_t(dpg[0], w1g[0, pl.ds(i * 256, 256), :])
        for j in range(1, 4):
            o = o + dot_t(dpg[j], w1g[j, pl.ds(i * 256, 256), :])
        dxs[i] = o.astype(BF).reshape(2, 4, 48, 256)
    for i in range(4):
        for d in range(2):
            dx, dk = (x + i) % 4, (k + d) % 2
            if i or d:
                put(dxs.at[dk, :, dx], dxr.at[x, k], dx1_r.at[x, k], (z, col(y, dx, dk)))
            else:
                keep(dxs.at[dk, :, dx], dxr.at[x, k], dx1_r.at[x, k])

    far_y = (y + 2) % 4
    for i in (2, 1, 3, 0):
        got(d2x.at[(y + i) % 4], d2x_r.at[(y + i) % 4])
    put(d2s.at[k, far_y], d2t.at[0], d2t_r.at[0], (z, col(up, x, k)))
    put(d2x.at[far_y], d2t.at[1], d2t_r.at[1], (z, col(down, x, k)))
    put(d2x.at[up], d2r.at[0, 1], d2_r.at[0, 1], (z, col(up, x, k)))
    put(d2s.at[k, down], d2r.at[1, 0], d2_r.at[1, 0], (z, col(down, x, k)))

    def part_w1(i, _):
        for r in range(2):
            d1s[i, pl.ds(r * 256, 256), :] = t_dot(xg[r].reshape(384, 256), dpg[i]).astype(BF)
        total = jnp.sum(dpg[i].astype(F32), axis=0, keepdims=True)
        bs[i] = jnp.broadcast_to(total, (8, 384))
        return 0

    lax.fori_loop(0, 4, part_w1, 0)
    low, high = pl.ds(0, 256), pl.ds(256, 256)
    for d, (dy, rows) in enumerate(((up, low), (down, high))):
        put(d1s.at[(y + 2) % 4, rows], d1t.at[d], d1t_r.at[d], (z, col(dy, x, k)))
    for d, (dy, rows) in enumerate(((up, high), (down, low))):
        put(d1s.at[dy, rows], d1r.at[d, rows], d1_r.at[d, 0], (z, col(dy, x, k)))
    keep(bs.at[y], dbr.at[y], db_r.at[y])
    for i in (1, 3, 2):
        dy = (y + i) % 4
        put(bs.at[dy], dbr.at[y], db_r.at[y], (z, col(dy, x, k)))

    for i in range(4):
        got(ya.at[i], y1_r.at[i])
    for i in range(8):
        j = (z + i) % 8
        rows = pl.ds(pl.multiple_of(j % 2 * 192, 192), 192)
        if i:
            put(ya.at[j // 2, rows], yr.at[z], y2_r.at[z], (j, c))
        else:
            keep(ya.at[j // 2, rows], yr.at[z], y2_r.at[z])

    for d in range(2):
        got(d2t.at[d], d2t_r.at[d])
    d2s[k, up] = d2s[k, up] + d2t[0]
    put(d2s.at[k, up], d2r.at[0, 0], d2_r.at[0, 0], (z, col(up, x, k)))
    d2x[down] = d2x[down] + d2t[1]
    put(d2x.at[down], d2r.at[1, 1], d2_r.at[1, 1], (z, col(down, x, k)))

    for d, (dy, rows) in enumerate(((up, low), (down, high))):
        got(d1t.at[d], d1t_r.at[d])
        d1s[dy, rows, :] = d1s[dy, rows, :] + d1t[d]
        put(d1s.at[dy, rows], d1r.at[d, rows], d1_r.at[d, 1], (z, col(dy, x, k)))

    for i in range(4):
        for d in range(2):
            got(dxr.at[i, d], dx1_r.at[i, d])
    for h in range(2):
        o = dxr[0, 0, h].astype(F32)
        for j in range(1, 8):
            o = o + dxr[j // 2, j % 2, h].astype(F32)
        for d in range(2):
            dxb[h, d] = o[:, d * 128:(d + 1) * 128].astype(BF)
    for h in range(2):
        for d in range(2):
            dev = back[2 * h + d]
            put_any(
                dxb.at[h, d], ot.at[x], dx2_r.at[x], dev,
                jnp.logical_and(dev[0] == z, dev[1] == c),
            )

    for i in range(2):
        for d in range(2):
            got(d2r.at[i, d], d2_r.at[i, d])

    def sum_w2(i, _):
        rows = pl.ds(pl.multiple_of(i * 64, 64), 64)
        for d, local in enumerate((d2s.at[k, y], d2x.at[y])):
            o = local[rows, :].astype(F32)
            for j in range(2):
                o = o + d2r[j, d, rows, :].astype(F32)
            start = (k if d == 0 else 1 - k) * 768 + i * 64
            out_w2[pl.ds(pl.multiple_of(start, 64), 64), :] = o
        return 0

    lax.fori_loop(0, 12, sum_w2, 0)
    for i in range(8):
        got(yr.at[i], y2_r.at[i])
    o = yr[0].astype(F32)
    for j in range(1, 8):
        o = o + yr[j].astype(F32)
    out_y[...] = o.astype(BF)
    for i in range(4):
        got(ot.at[i], dx2_r.at[i])
    out_x[...] = ot[...].reshape(192, 128)
    for i in range(4):
        got(dbr.at[i], db_r.at[i])
    for d, rows in enumerate((high, low)):
        got(d1r.at[d, rows], d1_r.at[d, 0])
        rest = low if d == 0 else high
        got(d1r.at[d, rest], d1_r.at[d, 1])

    def sum_w1(i, _):
        rows = pl.ds(pl.multiple_of(i * 32, 32), 32)
        o = d1s[y, rows, :].astype(F32)
        for j in range(2):
            o = o + d1r[j, rows, :].astype(F32)
        out_w1[rows, :] = o
        return 0

    lax.fori_loop(0, 16, sum_w1, 0)
    o = dbr[0] + dbr[1] + dbr[2] + dbr[3]
    out_b[...] = o[:1]

    for i, (like, cond) in enumerate(sent):
        ref = like()
        wait = pltpu.make_async_copy(ref, ref, send.at[i]).wait
        if cond is None:
            wait()
        else:
            pl.when(cond)(wait)


SENDS = 220
DMA = pltpu.SemaphoreType.DMA


def per_device(tokens, w_in, bias_in, w_out, grad_out):
    vm = pltpu.VMEM
    spec = pl.BlockSpec(memory_space=pltpu.VMEM)
    shapes = [
        ((192, 128), BF), ((192, 128), BF), ((512, 384), F32), ((1, 384), F32), ((1536, 128), F32),
    ]
    out = pl.pallas_call(
        kernel,
        out_shape=[jax.ShapeDtypeStruct(s, d) for s, d in shapes],
        in_specs=[spec] * 5,
        out_specs=[spec] * 5,
        scratch_shapes=[
            vm((2, 48, 256), BF),
            vm((2, 2, 4, 48, 256), BF),
            vm((4, 512, 384), BF),
            vm((768, 128), BF),
            vm((2, 768, 512), BF),
            vm((8, 192, 128), BF),
            vm((2, 2, 192, 512), BF),
            vm((8, 384), F32),
            vm((4, 8, 384), F32),
            vm((4, 384, 384), BF),
            vm((2, 2, 384, 384), BF),
            vm((2, 2, 384, 384), BF),
            vm((2, 384, 384), BF),
            vm((4, 384, 384), BF),
            vm((384, 384), BF),
            vm((2, 384, 384), BF),
            vm((4, 384, 384), BF),
            vm((2, 4, 384, 128), BF),
            vm((4, 384, 128), BF),
            vm((4, 384, 128), BF),
            vm((8, 192, 128), BF),
            vm((2, 4, 768, 128), BF),
            vm((4, 768, 128), BF),
            vm((2, 768, 128), BF),
            vm((2, 2, 768, 128), BF),
            vm((2, 2, 4, 48, 256), BF),
            vm((4, 2, 2, 48, 256), BF),
            vm((2, 2, 48, 128), BF),
            vm((4, 48, 128), BF),
            vm((4, 512, 384), BF),
            vm((2, 256, 384), BF),
            vm((2, 512, 384), BF),
            vm((4, 8, 384), F32),
            vm((4, 8, 384), F32),
            DMA((SENDS,)),
            DMA((2, 2)), DMA((4, 2)), DMA((4, 2)), DMA, DMA, DMA((4, 2, 2)), DMA((4,)),
            DMA((8,)), DMA((4,)), DMA, DMA((2, 2, 4)), DMA((4,)), DMA((2,)), DMA((4, 4)),
            DMA, DMA((4,)), DMA((8,)), DMA((4,)), DMA((2,)), DMA((2, 2)), DMA((4, 2)), DMA((4,)),
            DMA((2,)), DMA((2, 2)), DMA((4,)),
        ],
        compiler_params=pltpu.CompilerParams(
            collective_id=0, has_side_effects=True, vmem_limit_bytes=56 * 2**20
        ),
        name="mlp_grad",
    )(tokens, w_in, bias_in.reshape(1, 384), w_out, grad_out)
    block_out, grad_tokens, grad_w_in, grad_bias, grad_w_out = out
    return block_out, grad_tokens, grad_w_in, grad_bias.reshape(384), grad_w_out


def solution(mesh):
    return jax.shard_map(
        per_device,
        mesh=mesh,
        in_specs=(P("row", "col"), P("row", "col"), P("col"), P("row", "col"), P("row", "col")),
        out_specs=(P("row", "col"), P("row", "col"), P("row", "col"), P("col"), P("row", "col")),
        check_vma=False,
    )
```

time: 171 us -> 123 us (0.72)
  Pallas kernels: 162 us -> 114 us
    pallas_call x1, Pallas kernels: 162 us -> 114 us  [per_device(): pl.pallas_call(kernel, out_shape=[jax.ShapeDtypeStruct(s, d) for s, d in...]
where the time goes in v2:
time: 123 us; the launch traced here: 122 us
  Pallas kernels  114 us (93%)
  local copies, waits for them, and re-layouts  6.97 us (6%)
    pallas_call x1, Pallas kernels, per_device(): pl.pallas_call(kernel, out_shape=[jax.ShapeDtypeStruct(s, d) for s, d in...  114 us
    unnamed x10, local copies, waits for them, and re-layouts  5.73 us

profile of v2, /device:TPU:96, one launch (start us, length us, event | category | flops | bytes accessed | tf_op | source)
XLA Modules:
  0.0 122.2 jit_solution(14019236712369228350)
XLA Ops:
  0.6 1.2 %reshape.16.bias = f32[1,384]{1,0:T(1,128)} reshape(f32[384]{0:T(512)} %param.7) | data formatting | bytes 3072 | tf_op jit(solution)/shard_map/reshape | solution.py:536
  1.9 113.9 %mlp_grad.1 = (bf16[192,128]{1,0:T(8,128)(2,1)}, bf16[192,128]{1,0:T(8,128)(2,1)}, f32[512,384]{1,0:T(8,128)}, f32[1,384]{1,0:T(1,128)}, f32[1536,128]{1,0:T(8,128)}) custom-call(bf16[192,128]{1,0:T(8,128)(2,1)} %tok.1, bf16[512,384]{1,0:T(8,128)(2,1)} %w1.1, f32[1,384]{1,0:T(1,128)} %reshape.16.bias, bf16[1536,128]{1,0:T(8,128)(2,1)} %w2.1, bf16[192,128]{1,0:T(8,128)(2,1)} %go.1), custom_call_target="tpu_custom_call" | custom-call | tf_op jit(solution)/shard_map/mlp_grad/pallas_call | solution.py:486
  115.8 0.0 copy-start.2
  115.8 0.7 copy-done.2
  116.5 0.6 reduce
  117.1 0.0 copy-start.1
  117.1 1.4 %copy.14 = bf16[192,128]{1,0:T(8,128)(2,1)} copy(bf16[192,128]{1,0:T(8,128)(2,1)} %get-tuple-element.20) | data formatting | bytes 98304
  118.5 0.0 copy-done.1
  118.5 0.6 copy.15
  119.1 0.0 copy-start
  119.1 2.1 %copy.16 = f32[512,384]{1,0:T(8,128)} copy(f32[512,384]{1,0:T(8,128)} %get-tuple-element.22) | data formatting | bytes 1572864
  121.3 0.0 copy-done
  121.3 0.9 copy.17
Async XLA Ops:
  115.8 0.7 copy-start.2
  117.1 1.4 %copy-start.1 = (bf16[192,128]{1,0:T(8,128)(2,1)S(1)}, bf16[192,128]{1,0:T(8,128)(2,1)}, u32[]{:S(2)}) copy-start(bf16[192,128]{1,0:T(8,128)(2,1)} %get-tuple-element.21) | copy-start | bytes 147460
  119.1 2.1 %copy-start = (f32[1536,128]{1,0:T(8,128)S(1)}, f32[1536,128]{1,0:T(8,128)}, u32[]{:S(2)}) copy-start(f32[1536,128]{1,0:T(8,128)} %get-tuple-element.24) | copy-start | bytes 2359300

commit v3 on v2

--- a/solution.py
+++ b/solution.py
@@ -38,9 +38,9 @@
     out_y, out_x, out_w1, out_b, out_w2,
     xa, xg, w1g, w2h, w2g, gs, gg, b8, bg,
     ps, rz, tz, dhs, dhr, ho, hg, dpg,
-    ys, yx, ya, yr, d2s, d2x, d2t, d2r, dxs, dxr, dxb, ot, d1s, d1t, d1r, bs, dbr,
+    ys, yx, ya, yr, d2s, d2x, d2t, d2r, dxs, dxr, dxb, ot, d1s, d1t, d1r, bs, dbr, r_y, r_w1, r_w2, r_b,
     send, x1_r, x2_r, w1_r, w2s_r, w2k_r, w2_r, b_r, g1_r, g2_r, g3_r, p_r, dh_r, h_r, dp_r,
-    yx_r, y1_r, y2_r, d2x_r, d2t_r, d2_r, dx1_r, dx2_r, d1t_r, d1_r, db_r,
+    yx_r, y1_r, y2_r, d2x_r, d2t_r, d2_r, dx1_r, dx2_r, d1t_r, d1_r, db_r, out_r,
 ):
     z, c = lax.axis_index("row"), lax.axis_index("col")
     k, x, y = c % 2, (c // 2) % 4, c // 8
@@ -86,7 +86,7 @@
     for i in (4, 3, 5, 2, 6, 1, 7):
         put(go, gs.at[z], g1_r.at[z], ((z + i) % 8, c))
     up, down = (y + 1) % 4, (y + 3) % 4
-    b8[...] = jnp.broadcast_to(bias[...], b8.shape)
+    b8[...] = jnp.broadcast_to(bias[...].reshape(1, 384), b8.shape)
     for i in range(2):
         rows = pl.ds(i * 256, 256)
         keep(w1.at[rows], w1g.at[y, rows], w1_r.at[y, i])
@@ -116,7 +116,8 @@
         put(w1g.at[fy, rows], w1g.at[fy, rows], w1_r.at[fy, i], (z, col(dy, x, k)))
     got(w2h, w2s_r)
     keep(w2h, w2g.at[1 - k, :, lanes(y, 128)], w2s_r)
-    for i in range(2):
+
+    def start_w2(i):
         for dy in (up, down):
             rows = pl.ds(pl.multiple_of(k * 768 + i * 384, 384), 384)
             put(
@@ -129,6 +130,8 @@
                 (z, col(dy, x, k)),
             )
 
+    start_w2(0)
+
     def pass_w2(i):
         for d, (dy, fy) in enumerate(((up, down), (down, up))):
             block = w2g.at[d, pl.ds(i * 384, 384), lanes(fy, 128)]
@@ -215,33 +218,41 @@
         got(gg.at[k, :, :, pl.ds(i * 128, 128)], g2_r.at[i])
     put(gg.at[k], gg.at[k], g3_r, (z, col(y, x, 1 - k)))
 
+    pass_w2(0)
+    start_w2(1)
+
     @pl.when(other)
     def _():
         for n in range(2):
             for _, q in ways:
                 relay(other, first[q], 0, 0, n, q)
 
+    @pl.when(owner)
+    def _():
+        for n in range(2):
+            for _, q in ways:
+                relay(owner, second[q], 0, 1, n, q)
+
+    got(gg.at[1 - k], g3_r)
     got(w2g.at[k, :, lanes(y, 128)], w2k_r)
     got(w2g.at[1 - k, :, lanes(y, 128)], w2s_r)
-    pass_w2(0)
+    part_hidden(0)
 
     @pl.when(owner)
     def _():
-        for n in range(4):
+        for n in range(2, 4):
             for _, q in ways:
                 relay(owner, second[q], 0, 1, n, q)
 
     pass_w2(1)
-
-    got(gg.at[1 - k], g3_r)
-    part_hidden(0)
-    part_hidden(1)
 
     @pl.when(other)
     def _():
         for n in range(4):
             for _, q in ways:
                 relay(other, second[q], 1, 1, n, q)
+
+    part_hidden(1)
 
     @pl.when(owner)
     def _():
@@ -290,6 +301,38 @@
             pltpu.make_async_copy(ho, hg.at[k], h_r.at[k]).start
         )
 
+    low, high = pl.ds(0, 256), pl.ds(256, 256)
+    w1_key = len(sent)
+    for rows in (low, high, high, low):
+        sent.append((lambda: d1t.at[0], None))
+
+    def part_w1(step):
+        b = block_at(step)
+        for r in range(2):
+            d1s[b, pl.ds(r * 256, 256), :] = t_dot(xg[r].reshape(384, 256), dpg[b]).astype(BF)
+        total = jnp.sum(dpg[b].astype(F32), axis=0, keepdims=True)
+        bs[b] = jnp.broadcast_to(total, (8, 384))
+        off = (b - y + 4) % 4
+
+        def go_on(key, rows, dst, sem, dy):
+            pltpu.make_async_remote_copy(
+                src_ref=d1s.at[b, rows], dst_ref=dst, send_sem=send.at[w1_key + key], recv_sem=sem,
+                device_id=(z, col(dy, x, k)), device_id_type=MESH,
+            ).start()
+
+        @pl.when(off == 2)
+        def _():
+            go_on(0, low, d1t.at[0], d1t_r.at[0], up)
+            go_on(1, high, d1t.at[1], d1t_r.at[1], down)
+
+        @pl.when(off == 1)
+        def _():
+            go_on(2, high, d1r.at[0, high], d1_r.at[0, 0], up)
+
+        @pl.when(off == 3)
+        def _():
+            go_on(3, low, d1r.at[1, low], d1_r.at[1, 0], down)
+
     def pass_on(cond, back_by, all_rows):
         for n in range(4):
             for s, q in ways:
@@ -300,43 +343,58 @@
                 if all_rows or n < 2:
                     put(block, block, sem, ahead[q], cond, lambda: dpg.at[0, piece(0)])
 
-    pl.when(other)(lambda: pass_on(other, 1, True))
-    pl.when(owner)(lambda: pass_on(owner, 2, True))
+    @pl.when(other)
+    def _():
+        pass_on(other, 1, True)
+        part_w1(1)
+        part_w1(-1)
+
+    @pl.when(owner)
+    def _():
+        part_w1(0)
+        pass_on(owner, 2, True)
+        part_w1(2)
+        part_w1(-2)
+
+    pl.when(other)(lambda: pass_on(other, 3, False))
 
     for i in range(2):
         got(hg.at[i], h_r.at[i])
 
-    def part_out(i):
+    def part_out(i, slot):
         o = dot(hg[0], w2g[i, :384, :]) + dot(hg[1], w2g[i, 384:, :])
-        return o.astype(BF)
-
-    o = part_out(1 - k)
-    for j in range(4):
-        ys[0, j] = o[:, j * 128:(j + 1) * 128]
+        for j in range(4):
+            ys[slot, j] = o[:, j * 128:(j + 1) * 128].astype(BF)
+
+    def part_w2(i):
+        g = gg[i].reshape(384, 512)
+        for r in range(2):
+            o = t_dot(hg[r], g)
+            for j in range(4):
+                d2s[i, j, pl.ds(r * 384, 384), :] = o[:, j * 128:(j + 1) * 128].astype(BF)
+
+    part_w2(1 - k)
+    for i in (2, 1, 3, 0):
+        j = (y + i) % 4
+        put(d2s.at[1 - k, j], d2x.at[j], d2x_r.at[j], (z, col(y, x, 1 - k)))
+    part_out(1 - k, 0)
     put(ys.at[0], yx, yx_r, (z, col(y, x, 1 - k)))
-    o = part_out(k)
-    for j in range(4):
-        ys[1, j] = o[:, j * 128:(j + 1) * 128]
-    pl.when(other)(lambda: pass_on(other, 3, False))
+    part_w2(k)
+    far_y = (y + 2) % 4
+    put(d2s.at[k, far_y], d2t.at[0], d2t_r.at[0], (z, col(up, x, k)))
+    got(d2x.at[far_y], d2x_r.at[far_y])
+    put(d2x.at[far_y], d2t.at[1], d2t_r.at[1], (z, col(down, x, k)))
+    part_out(k, 1)
     got(yx, yx_r)
     for j in range(4):
         ys[1, j] = ys[1, j] + yx[j]
     keep(ys.at[1, y], ya.at[y], y1_r.at[y])
     for i in (1, 3, 2):
         put(ys.at[1, (y + i) % 4], ya.at[y], y1_r.at[y], (z, col((y + i) % 4, x, k)))
-
-    def part_w2(i, _):
-        g = gg[i].reshape(384, 512)
-        for r in range(2):
-            o = t_dot(hg[r], g)
-            for j in range(4):
-                d2s[i, j, pl.ds(r * 384, 384), :] = o[:, j * 128:(j + 1) * 128].astype(BF)
-        return 0
-
-    lax.fori_loop(0, 2, part_w2, 0)
-    for i in (2, 1, 3, 0):
-        j = (y + i) % 4
-        put(d2s.at[1 - k, j], d2x.at[j], d2x_r.at[j], (z, col(y, x, 1 - k)))
+    for i in (1, 3, 0):
+        got(d2x.at[(y + i) % 4], d2x_r.at[(y + i) % 4])
+    put(d2x.at[up], d2r.at[0, 1], d2_r.at[0, 1], (z, col(up, x, k)))
+    put(d2s.at[k, down], d2r.at[1, 0], d2_r.at[1, 0], (z, col(down, x, k)))
 
     @pl.when(owner)
     def _():
@@ -356,27 +414,15 @@
             else:
                 keep(dxs.at[dk, :, dx], dxr.at[x, k], dx1_r.at[x, k])
 
-    far_y = (y + 2) % 4
-    for i in (2, 1, 3, 0):
-        got(d2x.at[(y + i) % 4], d2x_r.at[(y + i) % 4])
-    put(d2s.at[k, far_y], d2t.at[0], d2t_r.at[0], (z, col(up, x, k)))
-    put(d2x.at[far_y], d2t.at[1], d2t_r.at[1], (z, col(down, x, k)))
-    put(d2x.at[up], d2r.at[0, 1], d2_r.at[0, 1], (z, col(up, x, k)))
-    put(d2s.at[k, down], d2r.at[1, 0], d2_r.at[1, 0], (z, col(down, x, k)))
-
-    def part_w1(i, _):
-        for r in range(2):
-            d1s[i, pl.ds(r * 256, 256), :] = t_dot(xg[r].reshape(384, 256), dpg[i]).astype(BF)
-        total = jnp.sum(dpg[i].astype(F32), axis=0, keepdims=True)
-        bs[i] = jnp.broadcast_to(total, (8, 384))
-        return 0
-
-    lax.fori_loop(0, 4, part_w1, 0)
-    low, high = pl.ds(0, 256), pl.ds(256, 256)
-    for d, (dy, rows) in enumerate(((up, low), (down, high))):
-        put(d1s.at[(y + 2) % 4, rows], d1t.at[d], d1t_r.at[d], (z, col(dy, x, k)))
-    for d, (dy, rows) in enumerate(((up, high), (down, low))):
-        put(d1s.at[dy, rows], d1r.at[d, rows], d1_r.at[d, 0], (z, col(dy, x, k)))
+    @pl.when(owner)
+    def _():
+        part_w1(4)
+
+    @pl.when(other)
+    def _():
+        part_w1(3)
+        part_w1(-3)
+
     keep(bs.at[y], dbr.at[y], db_r.at[y])
     for i in (1, 3, 2):
         dy = (y + i) % 4
@@ -392,6 +438,23 @@
         else:
             keep(ya.at[j // 2, rows], yr.at[z], y2_r.at[z])
 
+    for i in range(4):
+        for d in range(2):
+            got(dxr.at[i, d], dx1_r.at[i, d])
+    for h in range(2):
+        o = dxr[0, 0, h].astype(F32)
+        for j in range(1, 8):
+            o = o + dxr[j // 2, j % 2, h].astype(F32)
+        for d in range(2):
+            dxb[h, d] = o[:, d * 128:(d + 1) * 128].astype(BF)
+    for h in range(2):
+        for d in range(2):
+            dev = back[2 * h + d]
+            put_any(
+                dxb.at[h, d], ot.at[lanes(x, 48)], dx2_r.at[x], dev,
+                jnp.logical_and(dev[0] == z, dev[1] == c),
+            )
+
     for d in range(2):
         got(d2t.at[d], d2t_r.at[d])
     d2s[k, up] = d2s[k, up] + d2t[0]
@@ -403,23 +466,6 @@
         got(d1t.at[d], d1t_r.at[d])
         d1s[dy, rows, :] = d1s[dy, rows, :] + d1t[d]
         put(d1s.at[dy, rows], d1r.at[d, rows], d1_r.at[d, 1], (z, col(dy, x, k)))
-
-    for i in range(4):
-        for d in range(2):
-            got(dxr.at[i, d], dx1_r.at[i, d])
-    for h in range(2):
-        o = dxr[0, 0, h].astype(F32)
-        for j in range(1, 8):
-            o = o + dxr[j // 2, j % 2, h].astype(F32)
-        for d in range(2):
-            dxb[h, d] = o[:, d * 128:(d + 1) * 128].astype(BF)
-    for h in range(2):
-        for d in range(2):
-            dev = back[2 * h + d]
-            put_any(
-                dxb.at[h, d], ot.at[x], dx2_r.at[x], dev,
-                jnp.logical_and(dev[0] == z, dev[1] == c),
-            )
 
     for i in range(2):
         for d in range(2):
@@ -432,19 +478,21 @@
             for j in range(2):
                 o = o + d2r[j, d, rows, :].astype(F32)
             start = (k if d == 0 else 1 - k) * 768 + i * 64
-            out_w2[pl.ds(pl.multiple_of(start, 64), 64), :] = o
+            r_w2[pl.ds(pl.multiple_of(start, 64), 64), :] = o
         return 0
 
     lax.fori_loop(0, 12, sum_w2, 0)
+    keep(r_w2, out_w2, out_r.at[0])
     for i in range(8):
         got(yr.at[i], y2_r.at[i])
     o = yr[0].astype(F32)
     for j in range(1, 8):
         o = o + yr[j].astype(F32)
-    out_y[...] = o.astype(BF)
-    for i in range(4):
-        got(ot.at[i], dx2_r.at[i])
-    out_x[...] = ot[...].reshape(192, 128)
+    r_y[...] = o.astype(BF)
+    keep(r_y, out_y, out_r.at[1])
+    for i in range(4):
+        got(ot.at[pl.ds(i * 48, 48)], dx2_r.at[i])
+    keep(ot, out_x, out_r.at[2])
     for i in range(4):
         got(dbr.at[i], db_r.at[i])
     for d, rows in enumerate((high, low)):
@@ -457,12 +505,15 @@
         o = d1s[y, rows, :].astype(F32)
         for j in range(2):
             o = o + d1r[j, rows, :].astype(F32)
-        out_w1[rows, :] = o
+        r_w1[rows, :] = o
         return 0
 
     lax.fori_loop(0, 16, sum_w1, 0)
-    o = dbr[0] + dbr[1] + dbr[2] + dbr[3]
-    out_b[...] = o[:1]
+    keep(r_w1, out_w1, out_r.at[3])
+    r_b[...] = dbr[0] + dbr[1] + dbr[2] + dbr[3]
+    keep(r_b, out_b, out_r.at[4])
+    for i, ref in enumerate((out_w2, out_y, out_x, out_w1, out_b)):
+        got(ref, out_r.at[i])
 
     for i, (like, cond) in enumerate(sent):
         ref = like()
@@ -473,6 +524,28 @@
             pl.when(cond)(wait)
 
 
+def hand_over(*refs):
+    stage, sems = refs[10:14], refs[14]
+    parts = []
+    for n, i in enumerate((2, 4, 0, 1)):
+        rows = refs[i].shape[0] // 2
+        for half in range(2):
+            at = pl.ds(half * rows, rows)
+            key = 2 * n + half
+            parts.append((
+                pltpu.make_async_copy(refs[i].at[at], stage[n].at[at], sems.at[0, key]),
+                pltpu.make_async_copy(stage[n].at[at], refs[5 + i].at[at], sems.at[1, key]),
+            ))
+    for into, _ in parts:
+        into.start()
+    refs[8][...] = refs[3][0]
+    for into, away in parts:
+        into.wait()
+        away.start()
+    for _, away in parts:
+        away.wait()
+
+
 SENDS = 220
 DMA = pltpu.SemaphoreType.DMA
 
@@ -480,14 +553,15 @@
 def per_device(tokens, w_in, bias_in, w_out, grad_out):
     vm = pltpu.VMEM
     spec = pl.BlockSpec(memory_space=pltpu.VMEM)
+    away = pl.BlockSpec(memory_space=pl.ANY)
     shapes = [
-        ((192, 128), BF), ((192, 128), BF), ((512, 384), F32), ((1, 384), F32), ((1536, 128), F32),
+        ((192, 128), BF), ((192, 128), BF), ((512, 384), F32), ((8, 384), F32), ((1536, 128), F32),
     ]
     out = pl.pallas_call(
         kernel,
         out_shape=[jax.ShapeDtypeStruct(s, d) for s, d in shapes],
-        in_specs=[spec] * 5,
-        out_specs=[spec] * 5,
+        in_specs=[away, away, spec, away, away],
+        out_specs=[away] * 5,
         scratch_shapes=[
             vm((2, 48, 256), BF),
             vm((2, 2, 4, 48, 256), BF),
@@ -517,25 +591,39 @@
             vm((2, 2, 4, 48, 256), BF),
             vm((4, 2, 2, 48, 256), BF),
             vm((2, 2, 48, 128), BF),
-            vm((4, 48, 128), BF),
+            vm((192, 128), BF),
             vm((4, 512, 384), BF),
             vm((2, 256, 384), BF),
             vm((2, 512, 384), BF),
             vm((4, 8, 384), F32),
             vm((4, 8, 384), F32),
+            vm((192, 128), BF),
+            vm((512, 384), F32),
+            vm((1536, 128), F32),
+            vm((8, 384), F32),
             DMA((SENDS,)),
             DMA((2, 2)), DMA((4, 2)), DMA((4, 2)), DMA, DMA, DMA((4, 2, 2)), DMA((4,)),
             DMA((8,)), DMA((4,)), DMA, DMA((2, 2, 4)), DMA((4,)), DMA((2,)), DMA((4, 4)),
             DMA, DMA((4,)), DMA((8,)), DMA((4,)), DMA((2,)), DMA((2, 2)), DMA((4, 2)), DMA((4,)),
-            DMA((2,)), DMA((2, 2)), DMA((4,)),
+            DMA((2,)), DMA((2, 2)), DMA((4,)), DMA((5,)),
         ],
         compiler_params=pltpu.CompilerParams(
             collective_id=0, has_side_effects=True, vmem_limit_bytes=56 * 2**20
         ),
         name="mlp_grad",
-    )(tokens, w_in, bias_in.reshape(1, 384), w_out, grad_out)
-    block_out, grad_tokens, grad_w_in, grad_bias, grad_w_out = out
-    return block_out, grad_tokens, grad_w_in, grad_bias.reshape(384), grad_w_out
+    )(tokens, w_in, bias_in, w_out, grad_out)
+    final = [s if i != 3 else ((384,), F32) for i, s in enumerate(shapes)]
+    places = [spec if i == 3 else away for i in range(5)]
+    return tuple(
+        pl.pallas_call(
+            hand_over,
+            out_shape=[jax.ShapeDtypeStruct(s, d) for s, d in final],
+            in_specs=places,
+            out_specs=places,
+            scratch_shapes=[vm(*shapes[i]) for i in (2, 4, 0, 1)] + [DMA((2, 8))],
+            name="hand_over",
+        )(*out)
+    )
 
 
 def solution(mesh):

time: 123 us -> 116 us (0.943)
  local copies, waits for them, and re-layouts: 6.97 us -> 0 us
    unnamed x10 -> x0, local copies, waits for them, and re-layouts: 5.73 us -> none
    pallas_call x0 -> x1, Pallas kernels: none -> 3.55 us  [per_device(): pl.pallas_call(hand_over, out_shape=[jax.ShapeDtypeStruct(s, d) for s, d...]
    pallas_call x1, Pallas kernels: 114 us -> 110 us  [per_device(): pl.pallas_call(kernel, out_shape=[jax.ShapeDtypeStruct(s, d) for s, d in...]
    reshape x1 -> x0, local copies, waits for them, and re-layouts: 1.25 us -> none  [per_device(): bias_in.reshape(1, 384)]
where the time goes in v3:
time: 116 us; the launch traced here: 115 us
  Pallas kernels  114 us (98%)
    pallas_call x1, Pallas kernels, per_device(): pl.pallas_call(kernel, out_shape=[jax.ShapeDtypeStruct(s, d) for s, d in...  110 us
    pallas_call x1, Pallas kernels, per_device(): pl.pallas_call(hand_over, out_shape=[jax.ShapeDtypeStruct(s, d) for s, d...  3.55 us

profile of v3, /device:TPU:96, one launch (start us, length us, event | category | flops | bytes accessed | tf_op | source)
XLA Modules:
  0.0 114.6 jit_solution(6535245470238881729)
XLA Ops:
  0.6 110.5 %mlp_grad.1 = (bf16[192,128]{1,0:T(8,128)(2,1)}, bf16[192,128]{1,0:T(8,128)(2,1)}, f32[512,384]{1,0:T(8,128)}, f32[8,384]{1,0:T(8,128)}, f32[1536,128]{1,0:T(8,128)}) custom-call(bf16[192,128]{1,0:T(8,128)(2,1)} %tok.1, bf16[512,384]{1,0:T(8,128)(2,1)} %w1.1, f32[384]{0:T(512)} %bias.1, bf16[1536,128]{1,0:T(8,128)(2,1)} %w2.1, bf16[192,128]{1,0:T(8,128)(2,1)} %go.1), custom_call_target="tpu_custom_call" | custom-call | tf_op jit(solution)/shard_map/mlp_grad/pallas_call | solution.py:560
  111.1 3.6 %hand_over.1 = (bf16[192,128]{1,0:T(8,128)(2,1)}, bf16[192,128]{1,0:T(8,128)(2,1)}, f32[512,384]{1,0:T(8,128)}, f32[384]{0:T(512)}, f32[1536,128]{1,0:T(8,128)}) custom-call(bf16[192,128]{1,0:T(8,128)(2,1)} %get-tuple-element.10.refs_0_, bf16[192,128]{1,0:T(8,128)(2,1)} %get-tuple-element.11.refs_1_, f32[512,384]{1,0:T(8,128)} %get-tuple-element.12.refs_2_, ...), custom_call_target="tpu_custom_call" | custom-call | tf_op jit(solution)/shard_map/hand_over/pallas_call | solution.py:618

commit v4 on v3

--- a/solution.py
+++ b/solution.py
@@ -301,6 +301,42 @@
             pltpu.make_async_copy(ho, hg.at[k], h_r.at[k]).start
         )
 
+    far_y = (y + 2) % 4
+
+    def half_rows(r):
+        return pl.ds(r * 384, 384)
+
+    def part_w2(i, r):
+        o = t_dot(hg[r], gg[i].reshape(384, 512))
+        for j in range(4):
+            d2s[i, j, half_rows(r), :] = o[:, j * 128:(j + 1) * 128].astype(BF)
+
+    def swap_w2(r):
+        for i in (2, 1, 3, 0):
+            j = (y + i) % 4
+            put(
+                d2s.at[1 - k, j, half_rows(r)], d2x.at[j, half_rows(r)], d2x_r.at[r, j],
+                (z, col(y, x, 1 - k)),
+            )
+
+    def hop_one_w2(r):
+        at = half_rows(r)
+        for i in (2, 1, 3, 0):
+            got(d2x.at[(y + i) % 4, at], d2x_r.at[r, (y + i) % 4])
+        put(d2s.at[k, far_y, at], d2t.at[0, at], d2t_r.at[r, 0], (z, col(up, x, k)))
+        put(d2x.at[far_y, at], d2t.at[1, at], d2t_r.at[r, 1], (z, col(down, x, k)))
+        put(d2x.at[up, at], d2r.at[0, 1, at], d2_r.at[r, 0, 1], (z, col(up, x, k)))
+        put(d2s.at[k, down, at], d2r.at[1, 0, at], d2_r.at[r, 1, 0], (z, col(down, x, k)))
+
+    def hop_two_w2(r):
+        at = half_rows(r)
+        for d in range(2):
+            got(d2t.at[d, at], d2t_r.at[r, d])
+        d2s[k, up, at, :] = d2s[k, up, at, :] + d2t[0, at, :]
+        put(d2s.at[k, up, at], d2r.at[0, 0, at], d2_r.at[r, 0, 0], (z, col(up, x, k)))
+        d2x[down, at, :] = d2x[down, at, :] + d2t[1, at, :]
+        put(d2x.at[down, at], d2r.at[1, 1, at], d2_r.at[r, 1, 1], (z, col(down, x, k)))
+
     low, high = pl.ds(0, 256), pl.ds(256, 256)
     w1_key = len(sent)
     for rows in (low, high, high, low):
@@ -356,45 +392,34 @@
         part_w1(2)
         part_w1(-2)
 
+    got(hg.at[0], h_r.at[0])
+    part_w2(1 - k, 0)
+    swap_w2(0)
+    part_w2(k, 0)
     pl.when(other)(lambda: pass_on(other, 3, False))
-
-    for i in range(2):
-        got(hg.at[i], h_r.at[i])
+    hop_one_w2(0)
+
+    got(hg.at[1], h_r.at[1])
 
     def part_out(i, slot):
         o = dot(hg[0], w2g[i, :384, :]) + dot(hg[1], w2g[i, 384:, :])
         for j in range(4):
             ys[slot, j] = o[:, j * 128:(j + 1) * 128].astype(BF)
 
-    def part_w2(i):
-        g = gg[i].reshape(384, 512)
-        for r in range(2):
-            o = t_dot(hg[r], g)
-            for j in range(4):
-                d2s[i, j, pl.ds(r * 384, 384), :] = o[:, j * 128:(j + 1) * 128].astype(BF)
-
-    part_w2(1 - k)
-    for i in (2, 1, 3, 0):
-        j = (y + i) % 4
-        put(d2s.at[1 - k, j], d2x.at[j], d2x_r.at[j], (z, col(y, x, 1 - k)))
+    part_w2(1 - k, 1)
+    swap_w2(1)
+    part_w2(k, 1)
     part_out(1 - k, 0)
     put(ys.at[0], yx, yx_r, (z, col(y, x, 1 - k)))
-    part_w2(k)
-    far_y = (y + 2) % 4
-    put(d2s.at[k, far_y], d2t.at[0], d2t_r.at[0], (z, col(up, x, k)))
-    got(d2x.at[far_y], d2x_r.at[far_y])
-    put(d2x.at[far_y], d2t.at[1], d2t_r.at[1], (z, col(down, x, k)))
+    hop_one_w2(1)
     part_out(k, 1)
+    hop_two_w2(0)
     got(yx, yx_r)
     for j in range(4):
         ys[1, j] = ys[1, j] + yx[j]
     keep(ys.at[1, y], ya.at[y], y1_r.at[y])
     for i in (1, 3, 2):
         put(ys.at[1, (y + i) % 4], ya.at[y], y1_r.at[y], (z, col((y + i) % 4, x, k)))
-    for i in (1, 3, 0):
-        got(d2x.at[(y + i) % 4], d2x_r.at[(y + i) % 4])
-    put(d2x.at[up], d2r.at[0, 1], d2_r.at[0, 1], (z, col(up, x, k)))
-    put(d2s.at[k, down], d2r.at[1, 0], d2_r.at[1, 0], (z, col(down, x, k)))
 
     @pl.when(owner)
     def _():
@@ -427,6 +452,8 @@
     for i in (1, 3, 2):
         dy = (y + i) % 4
         put(bs.at[dy], dbr.at[y], db_r.at[y], (z, col(dy, x, k)))
+
+    hop_two_w2(1)
 
     for i in range(4):
         got(ya.at[i], y1_r.at[i])
@@ -455,21 +482,15 @@
                 jnp.logical_and(dev[0] == z, dev[1] == c),
             )
 
-    for d in range(2):
-        got(d2t.at[d], d2t_r.at[d])
-    d2s[k, up] = d2s[k, up] + d2t[0]
-    put(d2s.at[k, up], d2r.at[0, 0], d2_r.at[0, 0], (z, col(up, x, k)))
-    d2x[down] = d2x[down] + d2t[1]
-    put(d2x.at[down], d2r.at[1, 1], d2_r.at[1, 1], (z, col(down, x, k)))
-
     for d, (dy, rows) in enumerate(((up, low), (down, high))):
         got(d1t.at[d], d1t_r.at[d])
         d1s[dy, rows, :] = d1s[dy, rows, :] + d1t[d]
         put(d1s.at[dy, rows], d1r.at[d, rows], d1_r.at[d, 1], (z, col(dy, x, k)))
 
-    for i in range(2):
-        for d in range(2):
-            got(d2r.at[i, d], d2_r.at[i, d])
+    for r in range(2):
+        for i in range(2):
+            for d in range(2):
+                got(d2r.at[i, d, half_rows(r)], d2_r.at[r, i, d])
 
     def sum_w2(i, _):
         rows = pl.ds(pl.multiple_of(i * 64, 64), 64)
@@ -546,7 +567,7 @@
         away.wait()
 
 
-SENDS = 220
+SENDS = 260
 DMA = pltpu.SemaphoreType.DMA
 
 
@@ -604,7 +625,7 @@
             DMA((SENDS,)),
             DMA((2, 2)), DMA((4, 2)), DMA((4, 2)), DMA, DMA, DMA((4, 2, 2)), DMA((4,)),
             DMA((8,)), DMA((4,)), DMA, DMA((2, 2, 4)), DMA((4,)), DMA((2,)), DMA((4, 4)),
-            DMA, DMA((4,)), DMA((8,)), DMA((4,)), DMA((2,)), DMA((2, 2)), DMA((4, 2)), DMA((4,)),
+            DMA, DMA((4,)), DMA((8,)), DMA((2, 4)), DMA((2, 2)), DMA((2, 2, 2)), DMA((4, 2)), DMA((4,)),
             DMA((2,)), DMA((2, 2)), DMA((4,)), DMA((5,)),
         ],
         compiler_params=pltpu.CompilerParams(

time: 116 us -> 114 us (0.983)
  Pallas kernels: 114 us -> 112 us
    pallas_call x1, Pallas kernels: 110 us -> 108 us  [per_device(): pl.pallas_call(kernel, out_shape=[jax.ShapeDtypeStruct(s, d) for s, d in...]
where the time goes in v4:
time: 114 us; the launch traced here: 113 us
  Pallas kernels  112 us (98%)
    pallas_call x1, Pallas kernels, per_device(): pl.pallas_call(kernel, out_shape=[jax.ShapeDtypeStruct(s, d) for s, d in...  108 us
    pallas_call x1, Pallas kernels, per_device(): pl.pallas_call(hand_over, out_shape=[jax.ShapeDtypeStruct(s, d) for s, d...  3.55 us

profile of v4, /device:TPU:96, one launch (start us, length us, event | category | flops | bytes accessed | tf_op | source)
XLA Modules:
  0.0 112.7 jit_solution(4979426012747787054)
XLA Ops:
  0.6 108.5 %mlp_grad.1 = (bf16[192,128]{1,0:T(8,128)(2,1)}, bf16[192,128]{1,0:T(8,128)(2,1)}, f32[512,384]{1,0:T(8,128)}, f32[8,384]{1,0:T(8,128)}, f32[1536,128]{1,0:T(8,128)}) custom-call(bf16[192,128]{1,0:T(8,128)(2,1)} %tok.1, bf16[512,384]{1,0:T(8,128)(2,1)} %w1.1, f32[384]{0:T(512)} %bias.1, bf16[1536,128]{1,0:T(8,128)(2,1)} %w2.1, bf16[192,128]{1,0:T(8,128)(2,1)} %go.1), custom_call_target="tpu_custom_call" | custom-call | tf_op jit(solution)/shard_map/mlp_grad/pallas_call | solution.py:581
  109.1 3.6 %hand_over.1 = (bf16[192,128]{1,0:T(8,128)(2,1)}, bf16[192,128]{1,0:T(8,128)(2,1)}, f32[512,384]{1,0:T(8,128)}, f32[384]{0:T(512)}, f32[1536,128]{1,0:T(8,128)}) custom-call(bf16[192,128]{1,0:T(8,128)(2,1)} %get-tuple-element.10.refs_0_, bf16[192,128]{1,0:T(8,128)(2,1)} %get-tuple-element.11.refs_1_, f32[512,384]{1,0:T(8,128)} %get-tuple-element.12.refs_2_, ...), custom_call_target="tpu_custom_call" | custom-call | tf_op jit(solution)/shard_map/hand_over/pallas_call | solution.py:639

commit v5 on v4

--- a/solution.py
+++ b/solution.py
@@ -281,17 +281,13 @@
             return 0
 
         lax.fori_loop(0, 24, point, 0)
-        for n in range(4):
-            for _, q in ways:
-                block = dpg.at[z // 2, piece(halves(q)[n])]
-                put(block, block, dp_r.at[z // 2, halves(q)[n]], ahead[q], owner, lambda: dpg.at[0, piece(0)])
 
     @pl.when(jnp.logical_not(owner))
     def _():
         for i in range(4):
             got(bg.at[i], b_r.at[i])
 
-    for i in range(4):
+    for i in (2, 1, 3, 0):
         here = jnp.logical_and((x + i) % 4 == x, x % 2 == k)
         put(
             ho, hg.at[k], h_r.at[k], (z, col(y, (x + i) % 4, x % 2)),
@@ -300,6 +296,13 @@
         pl.when(jnp.logical_and(owner, here))(
             pltpu.make_async_copy(ho, hg.at[k], h_r.at[k]).start
         )
+
+    @pl.when(owner)
+    def _():
+        for n in range(4):
+            for _, q in ways:
+                block = dpg.at[z // 2, piece(halves(q)[n])]
+                put(block, block, dp_r.at[z // 2, halves(q)[n]], ahead[q], owner, lambda: dpg.at[0, piece(0)])
 
     far_y = (y + 2) % 4
 

time: 114 us -> 114 us (level)
  no operation moved by 1% of the time
where the time goes in v5:
time: 114 us; the launch traced here: 112 us
  Pallas kernels  112 us (98%)
    pallas_call x1, Pallas kernels, per_device(): pl.pallas_call(kernel, out_shape=[jax.ShapeDtypeStruct(s, d) for s, d in...  108 us
    pallas_call x1, Pallas kernels, per_device(): pl.pallas_call(hand_over, out_shape=[jax.ShapeDtypeStruct(s, d) for s, d...  3.55 us

profile of v5, /device:TPU:96, one launch (start us, length us, event | category | flops | bytes accessed | tf_op | source)
XLA Modules:
  0.0 112.3 jit_solution(1770758230960445321)
XLA Ops:
  0.6 108.1 %mlp_grad.1 = (bf16[192,128]{1,0:T(8,128)(2,1)}, bf16[192,128]{1,0:T(8,128)(2,1)}, f32[512,384]{1,0:T(8,128)}, f32[8,384]{1,0:T(8,128)}, f32[1536,128]{1,0:T(8,128)}) custom-call(bf16[192,128]{1,0:T(8,128)(2,1)} %tok.1, bf16[512,384]{1,0:T(8,128)(2,1)} %w1.1, f32[384]{0:T(512)} %bias.1, bf16[1536,128]{1,0:T(8,128)(2,1)} %w2.1, bf16[192,128]{1,0:T(8,128)(2,1)} %go.1), custom_call_target="tpu_custom_call" | custom-call | tf_op jit(solution)/shard_map/mlp_grad/pallas_call | solution.py:584
  108.7 3.6 %hand_over.1 = (bf16[192,128]{1,0:T(8,128)(2,1)}, bf16[192,128]{1,0:T(8,128)(2,1)}, f32[512,384]{1,0:T(8,128)}, f32[384]{0:T(512)}, f32[1536,128]{1,0:T(8,128)}) custom-call(bf16[192,128]{1,0:T(8,128)(2,1)} %get-tuple-element.10.refs_0_, bf16[192,128]{1,0:T(8,128)(2,1)} %get-tuple-element.11.refs_1_, f32[512,384]{1,0:T(8,128)} %get-tuple-element.12.refs_2_, ...), custom_call_target="tpu_custom_call" | custom-call | tf_op jit(solution)/shard_map/hand_over/pallas_call | solution.py:642
